TPU v7x, 256 devices: a whole 4x4x8 slice. The times are simulated.
256 devices in a mesh: shot: 2 (over z_hi), tx: 8 (over z_lo, core), ty: 16 (over x, y).
Axes of the slice: x: 4, y: 4, z: 8 (z_hi: 2, z_lo: 4; z = z_hi * 4 + z_lo), core: 2. Of those that a mesh axis runs over, the one named last changes fastest.
Arguments:
- perturbation: float32 [128, 128, 256], P(('tx', 'ty')), may hold values from -6 to 6
- courant_sq: float32 [128, 256, 128], P('tx', 'ty'), may hold values from 0.08 to 0.3
- background_prev: float32 [2, 128, 256, 128], P('shot', 'tx', 'ty'), may hold values from -6 to 6
- background_now: float32 [2, 128, 256, 128], P('shot', 'tx', 'ty'), may hold values from -6 to 6
- born_prev: float32 [2, 128, 256, 128], P('shot', 'tx', 'ty'), may hold values from -6 to 6
- born_now: float32 [2, 128, 256, 128], P('shot', 'tx', 'ty'), may hold values from -6 to 6
- adjoint_next: float32 [2, 128, 256, 128], P('shot', 'tx', 'ty'), may hold values from -6 to 6
- adjoint_after: float32 [2, 128, 256, 128], P('shot', 'tx', 'ty'), may hold values from -6 to 6
- encode_bits: int32 [2, 256], P('shot'), may hold values from 0 to 1
- wavelet: float32 [4], replicated, may hold values from -4 to 4
- source_x: int32 [256], replicated, may hold values from 0 to 127
- source_y: int32 [256], replicated, may hold values from 0 to 255
- receiver_x: int32 [1024], replicated, may hold values from 0 to 127
- receiver_y: int32 [1024], replicated, may hold values from 0 to 255
Outputs:
- hessian_image: float32 [128, 128, 256], P(('tx', 'ty'), None, 'shot')
- adjoint_first: float32 [2, 128, 256, 128], P('shot', 'tx', 'ty')
- adjoint_second: float32 [2, 128, 256, 128], P('shot', 'tx', 'ty')
- born_last: float32 [2, 128, 256, 128], P('shot', 'tx', 'ty')
- born_before: float32 [2, 128, 256, 128], P('shot', 'tx', 'ty')
Inputs may be any that keep to these rules, and one draw needn't show every extreme that they name: `receiver_x`: several receivers may share a cell.
All inputs are finite; a program needn't handle non-finite values.
Results may differ from a plain program's by a relative error of at most 0.00024.
Values sent between devices are 32-bit elements; how exact they have to be, the bound alone decides.
No kernel may reach another device: no remote copies, remote signals or barrier semaphores. Data moves between devices by JAX's collectives and lax.ppermute only.
A program may use at most 128 MiB of HBM per device.

v0:
```python
import jax
import jax.numpy as jnp
from jax import lax
from jax.experimental import pallas as pl
from jax.experimental.pallas import tpu as pltpu
from jax.sharding import PartitionSpec as P

STEPS = 4
SRC_DEPTH = 4
REC_DEPTH = 2
NZ = 128
T = 16
D = 4
G = T + 2 * D
H = 8
E = T + 2 * H
PAD = 8
XO = 1
SH = 8
WIDTHS = (4, 4, 4, 4, 3, 3, 3)
OFFSETS = tuple(sum(WIDTHS[:i]) * G for i in range(len(WIDTHS)))
SHALLOW = (0, 1, 2, 4, 5)
SHALLOW_ROW = sum(WIDTHS) * G
STRIP_Y = (4 * T + 5, 8, NZ)
STRIP_X = (SHALLOW_ROW + len(SHALLOW) * E, NZ)
F32 = jnp.float32
VMEM = pl.BlockSpec(memory_space=pltpu.VMEM)
SMEM = pl.BlockSpec(memory_space=pltpu.SMEM)
HBM = pl.BlockSpec(memory_space=pltpu.HBM)


BUSY = pl.CostEstimate(flops=10**15, bytes_accessed=10**9, transcendentals=0)


def call(body, outs, specs, scratch=(), mib=32, cost=None):
    return pl.pallas_call(
        body,
        out_shape=outs,
        in_specs=specs,
        out_specs=jax.tree.map(lambda _: VMEM, outs),
        scratch_shapes=list(scratch),
        compiler_params=pltpu.CompilerParams(vmem_limit_bytes=mib and mib * 1024 * 1024),
        cost_estimate=cost,
    )


def lanes(shape):
    return lax.broadcasted_iota(jnp.int32, shape, len(shape) - 1)


def turn(piece, amount):
    amount = amount % NZ
    return pltpu.roll(piece, amount, len(piece.shape) - 1) if amount else piece


def pack_windows(plane_ref, out_ref, left, right):
    lane = lanes((8, NZ))
    sub = lax.broadcasted_iota(jnp.int32, (8, NZ), 0)
    zero = jnp.zeros((8, NZ), F32)
    for half, side in enumerate((left, right)):
        side[0:8, :] = zero
        side[136:144, :] = zero
        side[8:136, :] = plane_ref[:, NZ * half : NZ * half + NZ]

    def put(block, row, start, at, where=None):
        for half, side in enumerate((left, right)):
            lo = max(start, NZ * half)
            hi = min(start + 32, NZ * half + NZ)
            if lo >= hi:
                continue
            here = (lane >= at + lo - start) & (lane < at + hi - start)
            if where is not None:
                here = here & where
            block = jnp.where(here, turn(side[8 + row : 16 + row, :], at - start), block)
        return block

    for chip in range(4):
        for pair in range(8):
            rest = zero
            for odd in range(2):
                start = 16 * (2 * pair + odd) - 8
                main = zero
                for g in range(6):
                    row = 32 * chip - 8 + 8 * g
                    if row < 0 or row >= 128:
                        continue
                    if g < 4:
                        main = put(main, row, start, 32 * g)
                    else:
                        mine = (sub >= 4) if odd else (sub < 4)
                        rest = put(rest, row - 4 * odd, start, 32 * (g - 4), mine)
                        rest = put(rest, row + 4 - 4 * odd, start, 64 + 32 * (g - 4), mine)
                base = 24 * (8 * chip + pair)
                out_ref[base + 16 * odd : base + 16 * odd + 8, :] = main
            out_ref[base + 8 : base + 16, :] = rest


def split_windows(arrived, mine, other):
    core = parity()[0] == 1
    odd = parity()[1]
    lane = lanes((8, 128))
    for k in range(64):
        main = arrived[pl.ds(12 * k + 4 * odd, 8), :]
        rest = arrived[pl.ds(12 * k + 8 - 8 * odd, 4), :]
        rest = jnp.concatenate([turn(rest, 64), rest], 0)
        upper = jnp.where(lane < 64, turn(main, 64), rest)
        mine[8 * k : 8 * k + 8, :] = jnp.where(core, upper, main)
        other[8 * k : 8 * k + 8, :] = jnp.where(core, main, upper)


def parity():
    return lax.rem(lax.axis_index("tx"), 2), lax.rem(lax.axis_index("ty"), 2)


def strips(ref, e_ref, o_ref, row, k):
    odd = parity()[1] == 1
    low = ref[:, 0:4, :]
    high = ref[:, 12:16, :]
    e_ref[row : row + T, k : k + 4, :] = jnp.where(odd, low, high)
    o_ref[row : row + T, k : k + 4, :] = jnp.where(odd, high, low)


def shallow_strips(ref, e_ref, o_ref, row, shallow, at):
    odd = parity()[1] == 1
    lane = lanes((T, NZ))
    packed = ref[0]
    for x in range(1, T):
        packed = jnp.where(lane >= SH * x, turn(ref[x], SH * x), packed)
    shallow[at : at + T, :] = packed
    e_ref[row] = jnp.where(odd, packed[0:8], packed[8:16])
    o_ref[row] = jnp.where(odd, packed[8:16], packed[0:8])


def pack_fields(*refs):
    sources, (e_ref, o_ref, shallow), targets, sems = refs[:8], refs[8:11], refs[11:19], refs[19]
    copies = [pltpu.make_async_copy(a, b, sems.at[i]) for i, (a, b) in enumerate(zip(sources, targets))]
    for copy in copies:
        copy.start()
    for f, ref in enumerate(targets[:7]):
        copies[f].wait()
        strips(ref, e_ref, o_ref, T * (f // 2), 4 * (f % 2))
        if f in SHALLOW:
            i = SHALLOW.index(f)
            shallow_strips(ref, e_ref, o_ref, 4 * T + i, shallow, T * i)
    blank = jnp.zeros((T, 4, NZ), F32)
    e_ref[3 * T : 4 * T, 4:8, :] = blank
    o_ref[3 * T : 4 * T, 4:8, :] = blank
    copies[7].wait()


def beside_y(got, f, rows):
    odd = parity()[1] == 1
    slot, k = f // 2, 4 * (f % 2)
    a, b = (strip[rows(T * slot), k : k + 4, :] for strip in got)
    return jnp.where(odd, a, b), jnp.where(odd, b, a)


def shallow_beside_y(got, i):
    odd = parity()[1] == 1
    a, b = (strip[4 * T + i] for strip in got)
    return jnp.where(odd, a, b), jnp.where(odd, b, a)


def pack_x(*refs):
    fields, shallow, got, (e_ref, o_ref) = refs[:7], refs[7], refs[8:10], refs[10:]
    odd_x = parity()[0]
    for f, ref in enumerate(fields):
        width = WIDTHS[f]
        for low, out in ((odd_x, e_ref), (1 - odd_x, o_ref)):
            first = (1 - low) * (T - width)
            for i in range(width):
                x = first + i
                row = OFFSETS[f] + G * i
                below, above = beside_y(got, f, lambda start: start + x)
                out[row : row + 4, :] = below
                out[row + 4 : row + 20, :] = ref[x]
                out[row + 20 : row + 24, :] = above
    for i in range(len(SHALLOW)):
        row = SHALLOW_ROW + E * i
        below, above = shallow_beside_y(got, i)
        for out in (e_ref, o_ref):
            out[row : row + 8, :] = below
            out[row + 8 : row + 24, :] = shallow[T * i : T * i + T, :]
            out[row + 24 : row + 32, :] = above


def count_planes(wavelet, sx, sy, bits, rx, ry, src_ref, rec_ref, scale_ref):
    x0 = lax.axis_index("tx") * T - T
    y0 = lax.axis_index("ty") * T - H
    for t in range(STEPS):
        scale_ref[t : t + 1, :] = jnp.full((1, NZ), wavelet[t], F32)

    def rows(values):
        grid = lax.broadcasted_iota(jnp.int32, (E, values.shape[1]), 0) + y0
        return jnp.where(grid == values, 1.0, 0.0).astype(F32)

    dims = (((1,), (1,)), ((), ()))
    sign = (2 * bits[...] - 1).astype(F32)
    for values, ys, depth, weight, out in (
        (sx[...], sy[...], SRC_DEPTH, sign, src_ref),
        (rx[...], ry[...], REC_DEPTH, None, rec_ref),
    ):
        left = rows(ys)
        if weight is not None:
            left = left * weight
        grid = lax.broadcasted_iota(jnp.int32, (NZ, values.shape[1]), 0)
        here = grid % SH == depth
        for piece in range(3):
            hit = here & (grid // SH + (x0 + T * piece) == values)
            right = jnp.where(hit, 1.0, 0.0).astype(F32)
            out[piece] = lax.dot_general(left, right, dims, preferred_element_type=F32)


def laplace(ref, x, n, ys, ny):
    rows = pl.ds(x, n)
    lane = lanes((1, 1, NZ))
    center = ref[rows, pl.ds(ys, ny), :]
    total = ref[pl.ds(x + 1, n), pl.ds(ys, ny), :] + ref[pl.ds(x - 1, n), pl.ds(ys, ny), :]
    total = total + ref[rows, pl.ds(ys + 1, ny), :] + ref[rows, pl.ds(ys - 1, ny), :]
    down = jnp.where(lane == NZ - 1, 0.0, turn(center, -1))
    up = jnp.where(lane == 0, 0.0, turn(center, 1))
    return center, total + down + up - 6.0 * center


def shallow_laplace(ref):
    rows = pl.ds(PAD, E)
    lane = lanes((3, E, NZ))
    center = ref[:, rows, :]
    total = ref[:, pl.ds(PAD + 1, E), :] + ref[:, pl.ds(PAD - 1, E), :]
    total = total + jnp.where(lane % SH == SH - 1, 0.0, turn(center, -1))
    total = total + jnp.where(lane % SH == 0, 0.0, turn(center, 1))
    left = turn(center, SH)
    right = turn(center, -SH)
    none = jnp.zeros((1, E, NZ), F32)
    left = jnp.where(lane < SH, jnp.concatenate([none, left[0:2]], 0), left)
    right = jnp.where(lane >= NZ - SH, jnp.concatenate([right[1:3], none], 0), right)
    return center, total + left + right - 6.0 * center


def loop(start, blocks, n, body):
    def step(i, carry):
        body(XO + start + i * n)
        return carry

    lax.fori_loop(0, blocks, step, 0)


ALL_Y = pl.ds(PAD, G)
OWN_Y = pl.ds(PAD + D, T)
OWN_X = pl.ds(XO + D, T)
PLAN = ((0, 4, 6), (2, 5, 4), (3, 3, 6), (4, 4, 4))
WIDE = (G + 2 * XO, G + 2 * PAD, NZ)
FLAT = (G + 2 * XO, G, NZ)
LOW = (3, E + 2 * PAD, NZ)


def clear_ends(ref):
    blank = jnp.zeros((3, PAD, NZ), F32)
    ref[:, 0:PAD, :] = blank
    ref[:, PAD + E : PAD + E + PAD, :] = blank


def assemble(f, ref, ext, got, xe, xo):
    odd = parity()[0] == 1
    ext[OWN_X, OWN_Y, :] = ref[...]
    below, above = beside_y(got, f, lambda start: slice(start, start + T))
    ext[OWN_X, PAD : PAD + 4, :] = below
    ext[OWN_X, PAD + 20 : PAD + 24, :] = above
    width = WIDTHS[f]
    for i in range(width):
        rows = pl.ds(OFFSETS[f] + G * i, G)
        got_e = xe[rows, :]
        got_o = xo[rows, :]
        ext[XO + D - width + i, ALL_Y, :] = jnp.where(odd, got_e, got_o)
        ext[XO + D + T + i, ALL_Y, :] = jnp.where(odd, got_o, got_e)


def assemble_shallow(i, mine, ext, got, xe, xo):
    odd = parity()[0] == 1
    rows = pl.ds(SHALLOW_ROW + E * i, E)
    got_e = xe[rows, :]
    got_o = xo[rows, :]
    ext[0, PAD : PAD + E, :] = jnp.where(odd, got_e, got_o)
    ext[2, PAD : PAD + E, :] = jnp.where(odd, got_o, got_e)
    ext[1, PAD + H : PAD + H + T, :] = mine
    below, above = shallow_beside_y(got, i)
    ext[1, PAD : PAD + H, :] = below
    ext[1, PAD + H + T : PAD + E, :] = above


def background(x, n, scale, now, old, C, SF, t):
    rows = pl.ds(x, n)
    center, lap = laplace(now, x, n, PAD, G)
    accel = C[rows, ALL_Y, :] * lap + scale * SF[rows]
    if t < STEPS - 1:
        old[rows, ALL_Y, :] = 2.0 * center - old[rows, ALL_Y, :] + accel
    return accel


def place_sources(src, SF):
    short = lanes((G, NZ))
    for x in range(1, G - 1):
        piece, at = (x - D + T) // T, SH * ((x - D) % T)
        SF[XO + x] = jnp.where(short == SRC_DEPTH, turn(src[piece, 4:28, :], -at), 0.0)


def free(scales, *refs):
    fields, shallow, got, refs = refs[:7], refs[7], refs[8:10], refs[10:]
    xe, xo, src, SA, CS, BS0, BS1, first, second, IM = refs[:10]
    U0, U1, C, M0, M1, Q0, Q1, SF, A, US = refs[10:]
    rows = pl.ds(PAD, E)

    with jax.named_scope("assemble"):
        for f, ext in ((0, U0), (2, C), (3, M0), (4, U1), (6, M1)):
            assemble(f, fields[f], ext, got, xe, xo)
        for ext in (US.at[0], US.at[1], BS0, BS1):
            clear_ends(ext)
        for i, ext in enumerate((US.at[0], BS1, CS, US.at[1], BS0)):
            assemble_shallow(i, shallow[T * i : T * i + T, :], ext, got, xe, xo)
        place_sources(src, SF)

    with jax.named_scope("shallow"):
        for t in range(STEPS):
            now, old = US.at[t % 2], US.at[1 - t % 2]
            center, lap = shallow_laplace(now)
            accel = CS[:, rows, :] * lap + scales[t : t + 1, :][None] * src[...]
            SA[t] = accel
            if t < STEPS - 1:
                old[:, rows, :] = 2.0 * center - old[:, rows, :] + accel

    waves = (U1, U0)
    for t in range(STEPS):
        with jax.named_scope("forward"):
            old, now = waves
            scale = scales[t : t + 1, :][None]
            start, blocks, n = PLAN[t]

            def forward(x):
                A[t, pl.ds(x, n)] = background(x, n, scale, now, old, C, SF, t)

            loop(start, blocks, n, forward)
            waves = (now, old)

    def scaled(x):
        rows = pl.ds(x, 6)
        Q0[rows, ALL_Y, :] = C[rows, ALL_Y, :] * M0[rows, ALL_Y, :]

    loop(0, 4, 6, scaled)
    upcoming, latest, q_now, q_new = M0, M1, Q0, Q1
    for t in range(STEPS, 1, -1):
        with jax.named_scope("adjoint"):
            start, blocks, n = PLAN[STEPS - t]

            def back(x):
                rows = pl.ds(x, n)
                _, lap = laplace(q_now, x, n, PAD, G)
                current = 2.0 * upcoming[rows, ALL_Y, :] - latest[rows, ALL_Y, :] + lap
                latest[rows, ALL_Y, :] = current
                q_new[rows, ALL_Y, :] = C[rows, ALL_Y, :] * current

            loop(start, blocks, n, back)
            upcoming, latest = latest, upcoming
            q_now, q_new = q_new, q_now

            def gather(x):
                rows = pl.ds(x, 4)
                mine = pl.ds(x - XO - D, 4)
                product = A[t - 1, rows, D : D + T, :] * upcoming[rows, OWN_Y, :]
                IM[mine] = -product if t == STEPS else IM[mine] - product

            loop(D, 4, 4, gather)

    def finish(x):
        rows = pl.ds(x, 4)
        mine = pl.ds(x - XO - D, 4)
        _, lap = laplace(q_now, x, 4, PAD + D, T)
        ahead = upcoming[rows, OWN_Y, :]
        current = 2.0 * ahead - latest[rows, OWN_Y, :] + lap
        first[mine] = current
        second[mine] = ahead
        IM[mine] = IM[mine] - A[0, rows, D : D + T, :] * current

    loop(D, 4, 4, finish)


def meet(SA, CS, BS0, BS1, IM0, mine, got, rec, image, sent, BS, PS, QS, IM):
    rows = pl.ds(PAD, E)
    with jax.named_scope("turn"):
        core = parity()[0] == 1
        planes = [jnp.where(core, got[pl.ds(s, SH, stride=8), :], mine[pl.ds(s, SH, stride=8), :]) for s in range(8)]
        planes = jnp.concatenate(planes, 0)
        turned = jnp.concatenate([planes, jnp.zeros((64, NZ), F32)], 0).T
        parts = [turned[32 * g : 32 * g + 32, :] for g in range(4)]
        flat = lanes((E, NZ))
        PS[0] = turn(parts[0], 64)
        PS[1] = jnp.where(flat < 64, parts[1], turn(parts[2], 64))
        PS[2] = parts[3]

    with jax.named_scope("shallow"):
        for i in range(STEPS):
            clear_ends(BS.at[i])
        for i in range(2):
            clear_ends(QS.at[i])
        olds = (BS0, BS1, BS.at[0], BS.at[1], BS.at[2], BS.at[3])
        for t in range(STEPS):
            center, lap = shallow_laplace(olds[t + 1])
            olds[t + 2][:, rows, :] = (
                2.0 * center - olds[t][:, rows, :] + CS[:, rows, :] * lap - PS[...] * SA[t]
            )
        own = pl.ds(H, T)
        now = rec[...] * BS[3, :, rows, :]
        older = None
        delta = -SA[3, 1, own, :] * now[1, H : H + T, :]
        for t in (3, 2, 1):
            QS[t % 2, :, rows, :] = CS[:, rows, :] * now
            _, lap = shallow_laplace(QS.at[t % 2])
            new = 2.0 * now + lap + rec[...] * BS[t - 1, :, rows, :]
            if older is not None:
                new = new - older
            now, older = new, now
            delta = delta - SA[t - 1, 1, own, :] * now[1, H : H + T, :]
        sent[0] = now[1, H : H + T, :]
        sent[1] = older[1, H : H + T, :]

    with jax.named_scope("image"):
        here = lanes((T, NZ)) < SH
        for x in range(T):
            IM[x] = IM0[x] + jnp.where(here, turn(delta, -SH * x), 0.0)
        for half in range(2):
            turned = IM[8 * half : 8 * half + 8].reshape(128, NZ).T
            for shot in range(2):
                image[pl.ds(256 * shot + half, 128, stride=2), :] = turned


def born(scales, *refs):
    fields, got, refs = refs[:7], refs[7:9], refs[9:]
    xe, xo, src, near, far, first0, second0, sent, last, before, first, second, U0, U1, C, PT, B, SF = refs
    for f, ext in ((0, U0), (1, B.at[1]), (2, C), (4, U1), (5, B.at[0])):
        assemble(f, fields[f], ext, got, xe, xo)
    place_sources(src, SF)
    core = parity()[0] == 1
    for s in range(8):
        planes = []
        for k in range(4):
            rows = pl.ds(128 * k + s, T, stride=8)
            a, b = near[rows, :], far[rows, :]
            planes += [jnp.where(core, b, a), jnp.where(core, a, b)]
        turned = jnp.concatenate(planes, 0).T
        for g in range(4):
            PT[8 * g + s] = turned[32 * g : 32 * g + 32, :]
    waves = (U1, U0)
    for t in range(STEPS):
        old, now = waves
        scale = scales[t : t + 1, :][None]
        start, blocks, n = PLAN[t]

        def step(x):
            rows = pl.ds(x, n)
            accel = background(x, n, scale, now, old, C, SF, t)
            center, lap = laplace(B.at[t + 1], x, n, PAD, G)
            B[t + 2, rows, ALL_Y, :] = (
                2.0 * center - B[t, rows, ALL_Y, :] + C[rows, ALL_Y, :] * lap
                - PT[pl.ds(x - XO + 4, n), 4:28, :] * accel
            )

        loop(start, blocks, n, step)
        waves = (now, old)
    last[...] = B[STEPS + 1, OWN_X, OWN_Y, :]
    before[...] = B[STEPS, OWN_X, OWN_Y, :]
    here = lanes((T, NZ)) < SH
    for x in range(T):
        first[x] = first0[x] + jnp.where(here, turn(sent[0], -SH * x), 0.0)
        second[x] = second0[x] + jnp.where(here, turn(sent[1], -SH * x), 0.0)


def arrange(arrived, out):
    first = lax.axis_index("shot") * 16
    lane = lanes((8, NZ))
    for half in range(2):
        groups = []
        for j in range(8):
            groups.append(
                arrived[pl.ds(first + 2 * j + half, 8, stride=32), :]
                + arrived[pl.ds(first + 256 + 2 * j + half, 8, stride=32), :]
            )
        for k in range(8):
            line = jnp.zeros((8, NZ), F32)
            for j in range(8):
                line = jnp.where((lane >= 16 * j) & (lane < 16 * j + 16), turn(groups[j], 16 * j - 16 * k), line)
            out[pl.ds(8 * half + k, 8, stride=16), :] = line


def swap(cells, axis, odd):
    count = lax.axis_size(axis)
    pairs = [(i, ((i - odd) ^ 1) + odd) for i in range(odd, count - odd)]
    return lax.ppermute(cells, axis, pairs)


def per_device(
    perturbation, courant_sq, background_prev, background_now, born_prev, born_now,
    adjoint_next, adjoint_after, encode_bits, wavelet, source_x, source_y, receiver_x, receiver_y,
):
    shape = lambda *dims: jax.ShapeDtypeStruct(dims, F32)
    tile = (T, T, NZ)
    fields = [
        a.reshape(tile)
        for a in (background_now, born_now, courant_sq, adjoint_next, background_prev, born_prev, adjoint_after)
    ]

    strip = shape(*STRIP_Y)
    send_e, send_o, shallow, *fields, plane = call(
        pack_fields,
        (strip, strip, shape(5 * T, NZ)) + (shape(*tile),) * 7 + (shape(128, 256),),
        [HBM] * 8,
        [pltpu.SemaphoreType.DMA((8,))],
    )(*[pltpu.with_memory_space_constraint(a, pltpu.HBM) for a in (*fields, perturbation.reshape(128, 256))])
    got = (swap(send_e, "ty", 0), swap(send_o, "ty", 1))
    side = pltpu.VMEM((144, NZ), F32)
    blocks = call(pack_windows, shape(768, NZ), [VMEM], [side, side])(plane)
    groups = [[(2 * chip + core) * 16 + ty for chip in range(4) for ty in range(16)] for core in range(2)]
    windows = lax.all_to_all(
        blocks.reshape(192, 4, NZ), ("tx", "ty"), split_axis=0, concat_axis=0, tiled=True, axis_index_groups=groups
    ).reshape(768, NZ)
    pieces = shape(3, E, NZ)
    src, rec, scales = call(count_planes, (pieces, pieces, shape(8, NZ)), [SMEM] + [VMEM] * 5)(
        wavelet, source_x[None], source_y[None], encode_bits, receiver_x[None], receiver_y[None]
    )
    windows, src, rec, scales = lax.optimization_barrier((windows, src, rec, scales))
    near, other = call(split_windows, (shape(512, NZ), shape(512, NZ)), [VMEM])(windows)
    far = swap(other, "tx", 0)
    strip = shape(*STRIP_X)
    send_e, send_o = call(pack_x, (strip, strip), [VMEM] * 10, cost=BUSY)(*fields, shallow, *got)
    across = (swap(send_e, "tx", 0), swap(send_o, "tx", 1))
    one = lambda *dims: pltpu.VMEM(dims, F32)
    cells = shape(*tile)
    low = shape(*LOW)
    SA, CS, BS0, BS1, first, second, IM = call(
        free,
        (shape(STEPS, 3, E, NZ), low, low, low, cells, cells, cells),
        [VMEM] * 14,
        [one(*WIDE)] * 7 + [one(*FLAT), one(STEPS, *FLAT), one(2, *LOW)],
    )(scales, *fields, shallow, *got, *across, src)
    image, sent = call(
        meet,
        (shape(512, NZ), shape(2, T, NZ)),
        [VMEM] * 8,
        [one(4, *LOW), one(3, E, NZ), one(2, *LOW), one(*tile)],
    )(SA, CS, BS0, BS1, IM, near, far, rec)
    last, before, first, second = call(
        born,
        (cells, cells, cells, cells),
        [VMEM] * 18,
        [one(*WIDE)] * 3 + [one(E, E, NZ), one(STEPS + 2, *WIDE), one(*FLAT)],
    )(scales, *fields, *got, *across, src, near, far, first, second, sent)

    arrived = lax.all_to_all(
        image.reshape(256, 2, NZ), ("shot", "tx", "ty"), split_axis=0, concat_axis=0, tiled=True
    )
    hessian = call(arrange, shape(128, NZ), [VMEM])(arrived.reshape(512, NZ))
    return (hessian[None], first[None], second[None], last[None], before[None])


def solution(mesh):
    field = P("shot", "tx", "ty", None)
    placed = (
        P(("tx", "ty"), None, None),
        P("tx", "ty", None),
        field, field, field, field, field, field,
        P("shot", None),
        P(), P(), P(), P(), P(),
    )
    return jax.shard_map(
        per_device,
        mesh=mesh,
        in_specs=placed,
        out_specs=(P(("tx", "ty"), None, "shot"), field, field, field, field),
        check_vma=False,
    )
```

profile of v0, /device:TPU:1, one launch (start us, length us, event | category | flops | bytes accessed | tf_op | source)
XLA Modules:
  0.0 67.9 jit_solution(15552765196550431994)
XLA Ops:
  0.6 1.5 %shard_map.173 = (f32[69,8,128]{2,1,0:T(8,128)S(1)}, f32[69,8,128]{2,1,0:T(8,128)S(1)}, f32[80,128]{1,0:T(8,128)S(1)}, f32[16,16,128]{2,1,0:T(8,128)S(1)}, f32[1...) custom-call(f32[16,16,128]{2,1,0:T(8,128)} %bitcast.25, ...), custom_call_target="tpu_custom_call" | custom-call | tf_op jit(solution)/shard_map/pallas_call | solution.py:511
  2.2 2.2 %collective-permute-start = (f32[69,8,128]{2,1,0:T(8,128)S(1)}, f32[69,8,128]{2,1,0:T(8,128)S(1)}, u32[]{:S(2)}, u32[]{:S(2)}) collective-permute-start(f32[69,8,128]{2,1,0:T(8,128)S(1)} %get-tuple-element.53), channel_id=1, source_target_pairs={{0,1},{1,0},{2,3},{3,2},{4,5},{5,4},{6,7},{7,6},{8,9},{9,8},{10,11... | collective-permute-start | bytes 847880 | tf_op jit(solution)/shard_map/ppermute | solution.py:496
  4.4 0.7 collective-permute-start.1
  5.1 1.4 %shard_map.174 = f32[768,128]{1,0:T(8,128)} custom-call(f32[128,256]{1,0:T(8,128)S(1)} %get-tuple-element.40.plane_ref), custom_call_target="tpu_custom_call" | custom-call | tf_op jit(solution)/shard_map/pallas_call | solution.py:519
  6.4 13.6 %all-to-all-start = ((f32[192,4,128]{2,1,0:T(4,128)}), f32[192,4,128]{2,1,0:T(4,128)}, u32[]{:S(2)}, u32[]{:S(2)}) async-start(f32[192,4,128]{2,1,0:T(4,128)} %bitcast.7), calls=%async_computation | async-start | bytes 786432 | tf_op jit(solution)/shard_map/all_to_all | solution.py:521
  20.0 0.0 collective-permute-done.refs_8_.refs_7_
  20.0 0.0 collective-permute-done.1.refs_9_.refs_8_
  20.0 0.0 copy-start
  20.1 0.0 copy-start.1
  20.1 0.0 copy-start.2
  20.1 0.0 copy-start.3
  20.1 0.0 copy-start.4
  20.1 0.0 copy-start.5
  20.1 1.0 %shard_map.176 = (f32[760,128]{1,0:T(8,128)}, f32[760,128]{1,0:T(8,128)}) custom-call(f32[16,16,128]{2,1,0:T(8,128)S(1)} %get-tuple-element.45.refs_0_, f32[16,16,128]{2,1,0:T(8,128)S(1)} %get-tuple-element.46.refs_1_, f32[16,16,128]{2,1,0:T(8,128)S(1)} %get-tuple-element.47.refs_2_, f32[16,16,128]{2,1,0:T(8,128)S(1)} %get-tuple-element.48.refs_3_, ...), custom_call_target="tpu_custom_call" | custom-call | flops 999999986991104 | bytes 1000000000 | tf_op jit(solution)/shard_map/pallas_call | solution.py:532
  21.1 1.5 %collective-permute-start.2 = (f32[760,128]{1,0:T(8,128)}, f32[760,128]{1,0:T(8,128)S(1)}, u32[]{:S(2)}, u32[]{:S(2)}) collective-permute-start(f32[760,128]{1,0:T(8,128)} %get-tuple-element.55), channel_id=1, source_target_pairs={{0,16},{16,0},{32,48},{48,32},{64,80},{80,64},{96,112},{112,96},{1... | collective-permute-start | bytes 1167368 | tf_op jit(solution)/shard_map/ppermute | solution.py:496
  22.6 3.0 %collective-permute-start.3 = (f32[760,128]{1,0:T(8,128)}, f32[760,128]{1,0:T(8,128)S(1)}, u32[]{:S(2)}, u32[]{:S(2)}) collective-permute-start(f32[760,128]{1,0:T(8,128)} %get-tuple-element.56), channel_id=1, source_target_pairs={{16,32},{32,16},{48,64},{64,48},{80,96},{96,80},{17,33},{33,17},{4... | collective-permute-start | bytes 1167368 | tf_op jit(solution)/shard_map/ppermute | solution.py:496
  25.7 0.0 copy-done
  25.7 0.0 copy-done.1
  25.7 0.0 copy-done.2
  25.7 1.0 %shard_map.175 = (f32[3,32,128]{2,1,0:T(8,128)S(1)}, f32[3,32,128]{2,1,0:T(8,128)S(1)}, f32[8,128]{1,0:T(8,128)S(1)}) custom-call(f32[4]{0:T(128)S(1)} %copy-done.5, s32[1,256]{1,0:T(1,128)S(1)} %bitcast.23, s32[1,256]{1,0:T(1,128)S(1)} %bitcast.24, s32[1,256]{1,0:T(1,128)S(1)} %copy-done.4, s32[1,1024]{1,0:T(1,128)S(1)} %bitcast.21, s32[1,1024]{1,0:T(1,128)S(1)} %bitcast.22), custom_call_target="tpu_custom_call" | custom-call | tf_op jit(solution)/shard_map/pallas_call | solution.py:525
  26.7 5.8 %all-to-all-done = f32[192,4,128]{2,1,0:T(4,128)} async-done(((f32[192,4,128]{2,1,0:T(4,128)}), f32[192,4,128]{2,1,0:T(4,128)}, u32[]{:S(2)}, u32[]{:S(2)}) %all-to-all-start) | async-done | bytes 393248 | tf_op jit(solution)/shard_map/all_to_all | solution.py:521
  32.5 1.2 %shard_map.178 = (f32[512,128]{1,0:T(8,128)S(1)}, f32[512,128]{1,0:T(8,128)S(1)}) custom-call(f32[768,128]{1,0:T(8,128)} %bitcast.8.arrived), custom_call_target="tpu_custom_call" | custom-call | tf_op jit(solution)/shard_map/pallas_call | solution.py:529
  33.7 3.8 %collective-permute-start.4 = (f32[512,128]{1,0:T(8,128)S(1)}, f32[512,128]{1,0:T(8,128)S(1)}, u32[]{:S(2)}, u32[]{:S(2)}) collective-permute-start(f32[512,128]{1,0:T(8,128)S(1)} %get-tuple-element.65), channel_id=1, source_target_pairs={{0,16},{16,0},{32,48},{48,32},{64,80},{80,64},{96,112},{112,96},{1... | collective-permute-start | bytes 786440 | tf_op jit(solution)/shard_map/ppermute | solution.py:496
  37.5 0.0 collective-permute-done.2.refs_10_.refs_9_
  37.5 0.0 collective-permute-done.3.refs_11_.refs_10_
  37.5 4.1 %shard_map.177 = (f32[4,3,32,128]{3,2,1,0:T(8,128)S(1)}, f32[3,48,128]{2,1,0:T(8,128)S(1)}, f32[3,48,128]{2,1,0:T(8,128)S(1)}, f32[3,48,128]{2,1,0:T(8,128)S(1)}...) custom-call(f32[8,128]{1,0:T(8,128)S(1)} %get-tuple-element.44.scales, ...), custom_call_target="tpu_custom_call" | custom-call | tf_op jit(solution)/shard_map/pallas_call | solution.py:537
  41.5 0.0 collective-permute-done.4.got.refs_13_
  41.6 1.6 %shard_map.179 = (f32[512,128]{1,0:T(8,128)}, f32[2,16,128]{2,1,0:T(8,128)S(1)}) custom-call(f32[4,3,32,128]{3,2,1,0:T(8,128)S(1)} %get-tuple-element.58.SA, f32[3,48,128]{2,1,0:T(8,128)S(1)} %get-tuple-element.59.CS, f32[3,48,128]{2,1,0:T(8,128)S(1)} %get-tuple-element.60.BS0, f32[3,48,128]{2,1,0:T(8,128)S(1)} %get-tuple-element.61.BS1, ...), custom_call_target="tpu_custom_call" | custom-call | tf_op jit(solution)/shard_map/pallas_call | solution.py:543
  43.2 8.2 %all-to-all-start.1 = ((f32[256,2,128]{2,1,0:T(2,128)}), f32[256,2,128]{2,1,0:T(2,128)S(1)}, u32[]{:S(2)}, u32[]{:S(2)}) async-start(f32[256,2,128]{2,1,0:T(2,128)} %bitcast.13), calls=%async_computation.1 | async-start | bytes 524288 | tf_op jit(solution)/shard_map/all_to_all | solution.py:556
  51.4 3.5 %shard_map.181 = (f32[16,16,128]{2,1,0:T(8,128)}, f32[16,16,128]{2,1,0:T(8,128)}, f32[16,16,128]{2,1,0:T(8,128)}, f32[16,16,128]{2,1,0:T(8,128)}) custom-call(f32[8,128]{1,0:T(8,128)S(1)} %get-tuple-element.44.scales, f32[16,16,128]{2,1,0:T(8,128)S(1)} %get-tuple-element.45.refs_0_, f32[16,16,128]{2,1,0:T(8,128)S(1)} %get-tuple-element.46.refs_1_, ...), custom_call_target="tpu_custom_call" | custom-call | tf_op jit(solution)/shard_map/pallas_call | solution.py:549
  54.8 12.3 %all-to-all-done.1 = f32[256,2,128]{2,1,0:T(2,128)S(1)} async-done(((f32[256,2,128]{2,1,0:T(2,128)}), f32[256,2,128]{2,1,0:T(2,128)S(1)}, u32[]{:S(2)}, u32[]{:S(2)}) %all-to-all-start.1) | async-done | bytes 262176 | tf_op jit(solution)/shard_map/all_to_all | solution.py:556
  67.1 0.8 %shard_map.180 = f32[128,128]{1,0:T(8,128)} custom-call(f32[512,128]{1,0:T(8,128)S(1)} %bitcast.20), custom_call_target="tpu_custom_call" | custom-call | tf_op jit(solution)/shard_map/pallas_call | solution.py:559
  (3 shorter events, 0.0 us)
Async XLA Ops:
  2.2 17.8 %collective-permute-start = (f32[69,8,128]{2,1,0:T(8,128)S(1)}, f32[69,8,128]{2,1,0:T(8,128)S(1)}, u32[]{:S(2)}, u32[]{:S(2)}) collective-permute-start(f32[69,8,128]{2,1,0:T(8,128)S(1)} %get-tuple-element.53), channel_id=1, source_target_pairs={{0,1},{1,0},{2,3},{3,2},{4,5},{5,4},{6,7},{7,6},{8,9},{9,8},{10,11... | collective-permute-start | bytes 847880 | tf_op jit(solution)/shard_map/ppermute | solution.py:496
  4.4 15.6 %collective-permute-start.1 = (f32[69,8,128]{2,1,0:T(8,128)S(1)}, f32[69,8,128]{2,1,0:T(8,128)S(1)}, u32[]{:S(2)}, u32[]{:S(2)}) collective-permute-start(f32[69,8,128]{2,1,0:T(8,128)S(1)} %get-tuple-element.54), channel_id=1, source_target_pairs={{1,2},{2,1},{3,4},{4,3},{5,6},{6,5},{7,8},{8,7},{9,10},{10,9},{11,... | collective-permute-start | bytes 847880 | tf_op jit(solution)/shard_map/ppermute | solution.py:496
  6.4 26.0 %all-to-all-start = ((f32[192,4,128]{2,1,0:T(4,128)}), f32[192,4,128]{2,1,0:T(4,128)}, u32[]{:S(2)}, u32[]{:S(2)}) async-start(f32[192,4,128]{2,1,0:T(4,128)} %bitcast.7), calls=%async_computation | async-start | bytes 786432 | tf_op jit(solution)/shard_map/all_to_all | solution.py:521
  20.0 5.6 %copy-start = (s32[1024]{0:T(1024)S(1)}, s32[1024]{0:T(1024)}, u32[]{:S(2)}) copy-start(s32[1024]{0:T(1024)} %param.26) | copy-start | bytes 12292
  20.1 5.6 %copy-start.1 = (s32[1024]{0:T(1024)S(1)}, s32[1024]{0:T(1024)}, u32[]{:S(2)}) copy-start(s32[1024]{0:T(1024)} %param.27) | copy-start | bytes 12292
  20.1 5.6 %copy-start.2 = (s32[256]{0:T(256)S(1)}, s32[256]{0:T(256)}, u32[]{:S(2)}) copy-start(s32[256]{0:T(256)} %param.24) | copy-start | bytes 3076
  20.1 5.6 %copy-start.3 = (s32[256]{0:T(256)S(1)}, s32[256]{0:T(256)}, u32[]{:S(2)}) copy-start(s32[256]{0:T(256)} %param.25) | copy-start | bytes 3076
  20.1 5.6 %copy-start.4 = (s32[1,256]{1,0:T(1,128)S(1)}, s32[1,256]{1,0:T(1,128)}, u32[]{:S(2)}) copy-start(s32[1,256]{1,0:T(1,128)} %bits.1) | copy-start | bytes 3076
  20.1 5.6 %copy-start.5 = (f32[4]{0:T(128)S(1)}, f32[4]{0:T(128)}, u32[]{:S(2)}) copy-start(f32[4]{0:T(128)} %wavelet.1) | copy-start | bytes 52
  21.1 16.3 %collective-permute-start.2 = (f32[760,128]{1,0:T(8,128)}, f32[760,128]{1,0:T(8,128)S(1)}, u32[]{:S(2)}, u32[]{:S(2)}) collective-permute-start(f32[760,128]{1,0:T(8,128)} %get-tuple-element.55), channel_id=1, source_target_pairs={{0,16},{16,0},{32,48},{48,32},{64,80},{80,64},{96,112},{112,96},{1... | collective-permute-start | bytes 1167368 | tf_op jit(solution)/shard_map/ppermute | solution.py:496
  22.6 14.8 %collective-permute-start.3 = (f32[760,128]{1,0:T(8,128)}, f32[760,128]{1,0:T(8,128)S(1)}, u32[]{:S(2)}, u32[]{:S(2)}) collective-permute-start(f32[760,128]{1,0:T(8,128)} %get-tuple-element.56), channel_id=1, source_target_pairs={{16,32},{32,16},{48,64},{64,48},{80,96},{96,80},{17,33},{33,17},{4... | collective-permute-start | bytes 1167368 | tf_op jit(solution)/shard_map/ppermute | solution.py:496
  33.7 7.9 %collective-permute-start.4 = (f32[512,128]{1,0:T(8,128)S(1)}, f32[512,128]{1,0:T(8,128)S(1)}, u32[]{:S(2)}, u32[]{:S(2)}) collective-permute-start(f32[512,128]{1,0:T(8,128)S(1)} %get-tuple-element.65), channel_id=1, source_target_pairs={{0,16},{16,0},{32,48},{48,32},{64,80},{80,64},{96,112},{112,96},{1... | collective-permute-start | bytes 786440 | tf_op jit(solution)/shard_map/ppermute | solution.py:496
  43.2 23.9 %all-to-all-start.1 = ((f32[256,2,128]{2,1,0:T(2,128)}), f32[256,2,128]{2,1,0:T(2,128)S(1)}, u32[]{:S(2)}, u32[]{:S(2)}) async-start(f32[256,2,128]{2,1,0:T(2,128)} %bitcast.13), calls=%async_computation.1 | async-start | bytes 524288 | tf_op jit(solution)/shard_map/all_to_all | solution.py:556
where the time goes:
time: 68.2 us; the launch traced here: 67.9 us
  starting transfers between devices  33 us (48%)
  waiting for transfers between devices  18 us (26%)
  Pallas kernels  16.1 us (24%)
  between operations  0.81 us (1%)
    all_to_all x1, starting transfers between devices, per_device(): lax.all_to_all(blocks.reshape(192, 4, NZ), ('tx', 'ty'), split_axis=0, co...  13.6 us
    all_to_all x1, waiting for transfers between devices, per_device(): lax.all_to_all(image.reshape(256, 2, NZ), ('shot', 'tx', 'ty'), split_axi...  12.3 us
    ppermute x5, starting transfers between devices, swap(): return lax.ppermute(cells, axis, pairs)  11.2 us
    all_to_all x1, starting transfers between devices, per_device(): lax.all_to_all(image.reshape(256, 2, NZ), ('shot', 'tx', 'ty'), split_axi...  8.18 us
    all_to_all x1, waiting for transfers between devices, per_device(): lax.all_to_all(blocks.reshape(192, 4, NZ), ('tx', 'ty'), split_axis=0, co...  5.77 us
    pallas_call x1, Pallas kernels, per_device(): call(free, (shape(STEPS, 3, E, NZ), low, low, low, cells, cells, cells),...  4.07 us
    pallas_call x1, Pallas kernels, per_device(): call(born, (cells, cells, cells, cells), [VMEM] * 18, [one(*WIDE)] * 3 +...  3.46 us
    pallas_call x1, Pallas kernels, per_device(): call(meet, (shape(512, NZ), shape(2, T, NZ)), [VMEM] * 8, [one(4, *LOW),...  1.61 us
  transfers between devices with their start and end apart: 7, of which 2 were waited for; matrix products, arithmetic and copies ran while one was open for 0% of the time, Pallas kernels for 18%

commit v1 on v0

--- a/solution.py
+++ b/solution.py
@@ -32,7 +32,7 @@
 BUSY = pl.CostEstimate(flops=10**15, bytes_accessed=10**9, transcendentals=0)
 
 
-def call(body, outs, specs, scratch=(), mib=32, cost=None):
+def call(body, outs, specs, scratch=(), mib=20, cost=None):
     return pl.pallas_call(
         body,
         out_shape=outs,
@@ -238,11 +238,8 @@
 
 
 def loop(start, blocks, n, body):
-    def step(i, carry):
+    for i in range(blocks):
         body(XO + start + i * n)
-        return carry
-
-    lax.fori_loop(0, blocks, step, 0)
 
 
 ALL_Y = pl.ds(PAD, G)

time: 68.2 us -> 66 us (0.968)
  Pallas kernels: 16.1 us -> 12.7 us
  waiting for transfers between devices: 18 us -> 19.2 us
    pallas_call x1, Pallas kernels: 4.07 us -> 1.8 us  [per_device(): call(free, (shape(STEPS, 3, E, NZ), low, low, low, cells, cells, cells),...]
    all_to_all x1, waiting for transfers between devices: 12.3 us -> 13.4 us  [per_device(): lax.all_to_all(image.reshape(256, 2, NZ), ('shot', 'tx', 'ty'), split_axi...]
    pallas_call x1, Pallas kernels: 3.46 us -> 2.31 us  [per_device(): call(born, (cells, cells, cells, cells), [VMEM] * 18, [one(*WIDE)] * 3 +...]
  transfers between devices with their start and end apart: 7 -> 7, of which waited for: 2 -> 2; matrix products, arithmetic and copies ran while one was open for 0% -> 0% of each run, Pallas kernels for 18% -> 13%
where the time goes in v1:
time: 66 us; the launch traced here: 65.7 us
  starting transfers between devices  33 us (50%)
  waiting for transfers between devices  19.2 us (29%)
  Pallas kernels  12.7 us (19%)
  between operations  0.81 us (1%)
    all_to_all x1, starting transfers between devices, per_device(): lax.all_to_all(blocks.reshape(192, 4, NZ), ('tx', 'ty'), split_axis=0, co...  13.6 us
    all_to_all x1, waiting for transfers between devices, per_device(): lax.all_to_all(image.reshape(256, 2, NZ), ('shot', 'tx', 'ty'), split_axi...  13.4 us
    ppermute x5, starting transfers between devices, swap(): return lax.ppermute(cells, axis, pairs)  11.2 us
    all_to_all x1, starting transfers between devices, per_device(): lax.all_to_all(image.reshape(256, 2, NZ), ('shot', 'tx', 'ty'), split_axi...  8.18 us
    all_to_all x1, waiting for transfers between devices, per_device(): lax.all_to_all(blocks.reshape(192, 4, NZ), ('tx', 'ty'), split_axis=0, co...  5.77 us
    pallas_call x1, Pallas kernels, per_device(): call(born, (cells, cells, cells, cells), [VMEM] * 18, [one(*WIDE)] * 3 +...  2.31 us
    pallas_call x1, Pallas kernels, per_device(): call(free, (shape(STEPS, 3, E, NZ), low, low, low, cells, cells, cells),...  1.8 us
    pallas_call x1, Pallas kernels, per_device(): call(meet, (shape(512, NZ), shape(2, T, NZ)), [VMEM] * 8, [one(4, *LOW),...  1.61 us
  transfers between devices with their start and end apart: 7, of which 2 were waited for; matrix products, arithmetic and copies ran while one was open for 0% of the time, Pallas kernels for 13%

profile of v1, /device:TPU:1, one launch (start us, length us, event | category | flops | bytes accessed | tf_op | source)
XLA Modules:
  0.0 65.7 jit_solution(2558733338334461381)
XLA Ops:
  0.6 1.5 %shard_map.173 = (f32[69,8,128]{2,1,0:T(8,128)S(1)}, f32[69,8,128]{2,1,0:T(8,128)S(1)}, f32[80,128]{1,0:T(8,128)S(1)}, f32[16,16,128]{2,1,0:T(8,128)S(1)}, f32[1...) custom-call(f32[16,16,128]{2,1,0:T(8,128)} %bitcast.25, ...), custom_call_target="tpu_custom_call" | custom-call | tf_op jit(solution)/shard_map/pallas_call | solution.py:508
  2.2 2.2 %collective-permute-start = (f32[69,8,128]{2,1,0:T(8,128)S(1)}, f32[69,8,128]{2,1,0:T(8,128)S(1)}, u32[]{:S(2)}, u32[]{:S(2)}) collective-permute-start(f32[69,8,128]{2,1,0:T(8,128)S(1)} %get-tuple-element.53), channel_id=1, source_target_pairs={{0,1},{1,0},{2,3},{3,2},{4,5},{5,4},{6,7},{7,6},{8,9},{9,8},{10,11... | collective-permute-start | bytes 847880 | tf_op jit(solution)/shard_map/ppermute | solution.py:493
  4.4 0.7 %collective-permute-start.1 = (f32[69,8,128]{2,1,0:T(8,128)S(1)}, f32[69,8,128]{2,1,0:T(8,128)S(1)}, u32[]{:S(2)}, u32[]{:S(2)}) collective-permute-start(f32[69,8,128]{2,1,0:T(8,128)S(1)} %get-tuple-element.54), channel_id=1, source_target_pairs={{1,2},{2,1},{3,4},{4,3},{5,6},{6,5},{7,8},{8,7},{9,10},{10,9},{11,... | collective-permute-start | bytes 847880 | tf_op jit(solution)/shard_map/ppermute | solution.py:493
  5.1 1.4 %shard_map.174 = f32[768,128]{1,0:T(8,128)} custom-call(f32[128,256]{1,0:T(8,128)S(1)} %get-tuple-element.40.plane_ref), custom_call_target="tpu_custom_call" | custom-call | tf_op jit(solution)/shard_map/pallas_call | solution.py:516
  6.4 13.6 %all-to-all-start = ((f32[192,4,128]{2,1,0:T(4,128)}), f32[192,4,128]{2,1,0:T(4,128)}, u32[]{:S(2)}, u32[]{:S(2)}) async-start(f32[192,4,128]{2,1,0:T(4,128)} %bitcast.7), calls=%async_computation | async-start | bytes 786432 | tf_op jit(solution)/shard_map/all_to_all | solution.py:518
  20.0 0.0 collective-permute-done.refs_8_.refs_7_
  20.0 0.0 collective-permute-done.1.refs_9_.refs_8_
  20.0 0.0 copy-start
  20.1 0.0 copy-start.1
  20.1 0.0 copy-start.2
  20.1 0.0 copy-start.3
  20.1 0.0 copy-start.4
  20.1 0.0 copy-start.5
  20.1 1.0 %shard_map.176 = (f32[760,128]{1,0:T(8,128)}, f32[760,128]{1,0:T(8,128)}) custom-call(f32[16,16,128]{2,1,0:T(8,128)S(1)} %get-tuple-element.45.refs_0_, f32[16,16,128]{2,1,0:T(8,128)S(1)} %get-tuple-element.46.refs_1_, f32[16,16,128]{2,1,0:T(8,128)S(1)} %get-tuple-element.47.refs_2_, f32[16,16,128]{2,1,0:T(8,128)S(1)} %get-tuple-element.48.refs_3_, ...), custom_call_target="tpu_custom_call" | custom-call | flops 999999986991104 | bytes 1000000000 | tf_op jit(solution)/shard_map/pallas_call | solution.py:529
  21.1 1.5 %collective-permute-start.2 = (f32[760,128]{1,0:T(8,128)}, f32[760,128]{1,0:T(8,128)S(1)}, u32[]{:S(2)}, u32[]{:S(2)}) collective-permute-start(f32[760,128]{1,0:T(8,128)} %get-tuple-element.55), channel_id=1, source_target_pairs={{0,16},{16,0},{32,48},{48,32},{64,80},{80,64},{96,112},{112,96},{1... | collective-permute-start | bytes 1167368 | tf_op jit(solution)/shard_map/ppermute | solution.py:493
  22.6 3.0 %collective-permute-start.3 = (f32[760,128]{1,0:T(8,128)}, f32[760,128]{1,0:T(8,128)S(1)}, u32[]{:S(2)}, u32[]{:S(2)}) collective-permute-start(f32[760,128]{1,0:T(8,128)} %get-tuple-element.56), channel_id=1, source_target_pairs={{16,32},{32,16},{48,64},{64,48},{80,96},{96,80},{17,33},{33,17},{4... | collective-permute-start | bytes 1167368 | tf_op jit(solution)/shard_map/ppermute | solution.py:493
  25.7 0.0 copy-done
  25.7 0.0 copy-done.1
  25.7 0.0 copy-done.2
  25.7 1.0 %shard_map.175 = (f32[3,32,128]{2,1,0:T(8,128)S(1)}, f32[3,32,128]{2,1,0:T(8,128)S(1)}, f32[8,128]{1,0:T(8,128)S(1)}) custom-call(f32[4]{0:T(128)S(1)} %copy-done.5, s32[1,256]{1,0:T(1,128)S(1)} %bitcast.23, s32[1,256]{1,0:T(1,128)S(1)} %bitcast.24, s32[1,256]{1,0:T(1,128)S(1)} %copy-done.4, s32[1,1024]{1,0:T(1,128)S(1)} %bitcast.21, s32[1,1024]{1,0:T(1,128)S(1)} %bitcast.22), custom_call_target="tpu_custom_call" | custom-call | tf_op jit(solution)/shard_map/pallas_call | solution.py:522
  26.7 5.8 %all-to-all-done = f32[192,4,128]{2,1,0:T(4,128)} async-done(((f32[192,4,128]{2,1,0:T(4,128)}), f32[192,4,128]{2,1,0:T(4,128)}, u32[]{:S(2)}, u32[]{:S(2)}) %all-to-all-start) | async-done | bytes 393248 | tf_op jit(solution)/shard_map/all_to_all | solution.py:518
  32.5 1.2 %shard_map.178 = (f32[512,128]{1,0:T(8,128)S(1)}, f32[512,128]{1,0:T(8,128)S(1)}) custom-call(f32[768,128]{1,0:T(8,128)} %bitcast.8.arrived), custom_call_target="tpu_custom_call" | custom-call | tf_op jit(solution)/shard_map/pallas_call | solution.py:526
  33.7 3.8 %collective-permute-start.4 = (f32[512,128]{1,0:T(8,128)S(1)}, f32[512,128]{1,0:T(8,128)S(1)}, u32[]{:S(2)}, u32[]{:S(2)}) collective-permute-start(f32[512,128]{1,0:T(8,128)S(1)} %get-tuple-element.65), channel_id=1, source_target_pairs={{0,16},{16,0},{32,48},{48,32},{64,80},{80,64},{96,112},{112,96},{1... | collective-permute-start | bytes 786440 | tf_op jit(solution)/shard_map/ppermute | solution.py:493
  37.5 0.0 collective-permute-done.2.refs_10_.refs_9_
  37.5 0.0 collective-permute-done.3.refs_11_.refs_10_
  37.5 1.8 %shard_map.177 = (f32[4,3,32,128]{3,2,1,0:T(8,128)S(1)}, f32[3,48,128]{2,1,0:T(8,128)S(1)}, f32[3,48,128]{2,1,0:T(8,128)S(1)}, f32[3,48,128]{2,1,0:T(8,128)S(1)}...) custom-call(f32[8,128]{1,0:T(8,128)S(1)} %get-tuple-element.44.scales, ...), custom_call_target="tpu_custom_call" | custom-call | tf_op jit(solution)/shard_map/pallas_call | solution.py:534
  39.3 0.0 collective-permute-done.4.got.refs_13_
  39.3 1.6 %shard_map.179 = (f32[512,128]{1,0:T(8,128)}, f32[2,16,128]{2,1,0:T(8,128)S(1)}) custom-call(f32[4,3,32,128]{3,2,1,0:T(8,128)S(1)} %get-tuple-element.58.SA, f32[3,48,128]{2,1,0:T(8,128)S(1)} %get-tuple-element.59.CS, f32[3,48,128]{2,1,0:T(8,128)S(1)} %get-tuple-element.60.BS0, f32[3,48,128]{2,1,0:T(8,128)S(1)} %get-tuple-element.61.BS1, ...), custom_call_target="tpu_custom_call" | custom-call | tf_op jit(solution)/shard_map/pallas_call | solution.py:540
  40.9 8.2 %all-to-all-start.1 = ((f32[256,2,128]{2,1,0:T(2,128)}), f32[256,2,128]{2,1,0:T(2,128)S(1)}, u32[]{:S(2)}, u32[]{:S(2)}) async-start(f32[256,2,128]{2,1,0:T(2,128)} %bitcast.13), calls=%async_computation.1 | async-start | bytes 524288 | tf_op jit(solution)/shard_map/all_to_all | solution.py:553
  49.1 2.3 %shard_map.181 = (f32[16,16,128]{2,1,0:T(8,128)}, f32[16,16,128]{2,1,0:T(8,128)}, f32[16,16,128]{2,1,0:T(8,128)}, f32[16,16,128]{2,1,0:T(8,128)}) custom-call(f32[8,128]{1,0:T(8,128)S(1)} %get-tuple-element.44.scales, f32[16,16,128]{2,1,0:T(8,128)S(1)} %get-tuple-element.45.refs_0_, f32[16,16,128]{2,1,0:T(8,128)S(1)} %get-tuple-element.46.refs_1_, ...), custom_call_target="tpu_custom_call" | custom-call | tf_op jit(solution)/shard_map/pallas_call | solution.py:546
  51.4 13.4 %all-to-all-done.1 = f32[256,2,128]{2,1,0:T(2,128)S(1)} async-done(((f32[256,2,128]{2,1,0:T(2,128)}), f32[256,2,128]{2,1,0:T(2,128)S(1)}, u32[]{:S(2)}, u32[]{:S(2)}) %all-to-all-start.1) | async-done | bytes 262176 | tf_op jit(solution)/shard_map/all_to_all | solution.py:553
  64.8 0.8 %shard_map.180 = f32[128,128]{1,0:T(8,128)} custom-call(f32[512,128]{1,0:T(8,128)S(1)} %bitcast.20), custom_call_target="tpu_custom_call" | custom-call | tf_op jit(solution)/shard_map/pallas_call | solution.py:556
  (3 shorter events, 0.0 us)
Async XLA Ops:
  2.2 17.8 %collective-permute-start = (f32[69,8,128]{2,1,0:T(8,128)S(1)}, f32[69,8,128]{2,1,0:T(8,128)S(1)}, u32[]{:S(2)}, u32[]{:S(2)}) collective-permute-start(f32[69,8,128]{2,1,0:T(8,128)S(1)} %get-tuple-element.53), channel_id=1, source_target_pairs={{0,1},{1,0},{2,3},{3,2},{4,5},{5,4},{6,7},{7,6},{8,9},{9,8},{10,11... | collective-permute-start | bytes 847880 | tf_op jit(solution)/shard_map/ppermute | solution.py:493
  4.4 15.6 %collective-permute-start.1 = (f32[69,8,128]{2,1,0:T(8,128)S(1)}, f32[69,8,128]{2,1,0:T(8,128)S(1)}, u32[]{:S(2)}, u32[]{:S(2)}) collective-permute-start(f32[69,8,128]{2,1,0:T(8,128)S(1)} %get-tuple-element.54), channel_id=1, source_target_pairs={{1,2},{2,1},{3,4},{4,3},{5,6},{6,5},{7,8},{8,7},{9,10},{10,9},{11,... | collective-permute-start | bytes 847880 | tf_op jit(solution)/shard_map/ppermute | solution.py:493
  6.4 26.0 %all-to-all-start = ((f32[192,4,128]{2,1,0:T(4,128)}), f32[192,4,128]{2,1,0:T(4,128)}, u32[]{:S(2)}, u32[]{:S(2)}) async-start(f32[192,4,128]{2,1,0:T(4,128)} %bitcast.7), calls=%async_computation | async-start | bytes 786432 | tf_op jit(solution)/shard_map/all_to_all | solution.py:518
  20.0 5.6 %copy-start = (s32[1024]{0:T(1024)S(1)}, s32[1024]{0:T(1024)}, u32[]{:S(2)}) copy-start(s32[1024]{0:T(1024)} %param.26) | copy-start | bytes 12292
  20.1 5.6 %copy-start.1 = (s32[1024]{0:T(1024)S(1)}, s32[1024]{0:T(1024)}, u32[]{:S(2)}) copy-start(s32[1024]{0:T(1024)} %param.27) | copy-start | bytes 12292
  20.1 5.6 %copy-start.2 = (s32[256]{0:T(256)S(1)}, s32[256]{0:T(256)}, u32[]{:S(2)}) copy-start(s32[256]{0:T(256)} %param.24) | copy-start | bytes 3076
  20.1 5.6 %copy-start.3 = (s32[256]{0:T(256)S(1)}, s32[256]{0:T(256)}, u32[]{:S(2)}) copy-start(s32[256]{0:T(256)} %param.25) | copy-start | bytes 3076
  20.1 5.6 %copy-start.4 = (s32[1,256]{1,0:T(1,128)S(1)}, s32[1,256]{1,0:T(1,128)}, u32[]{:S(2)}) copy-start(s32[1,256]{1,0:T(1,128)} %bits.1) | copy-start | bytes 3076
  20.1 5.6 %copy-start.5 = (f32[4]{0:T(128)S(1)}, f32[4]{0:T(128)}, u32[]{:S(2)}) copy-start(f32[4]{0:T(128)} %wavelet.1) | copy-start | bytes 52
  21.1 16.3 %collective-permute-start.2 = (f32[760,128]{1,0:T(8,128)}, f32[760,128]{1,0:T(8,128)S(1)}, u32[]{:S(2)}, u32[]{:S(2)}) collective-permute-start(f32[760,128]{1,0:T(8,128)} %get-tuple-element.55), channel_id=1, source_target_pairs={{0,16},{16,0},{32,48},{48,32},{64,80},{80,64},{96,112},{112,96},{1... | collective-permute-start | bytes 1167368 | tf_op jit(solution)/shard_map/ppermute | solution.py:493
  22.6 14.8 %collective-permute-start.3 = (f32[760,128]{1,0:T(8,128)}, f32[760,128]{1,0:T(8,128)S(1)}, u32[]{:S(2)}, u32[]{:S(2)}) collective-permute-start(f32[760,128]{1,0:T(8,128)} %get-tuple-element.56), channel_id=1, source_target_pairs={{16,32},{32,16},{48,64},{64,48},{80,96},{96,80},{17,33},{33,17},{4... | collective-permute-start | bytes 1167368 | tf_op jit(solution)/shard_map/ppermute | solution.py:493
  33.7 5.6 %collective-permute-start.4 = (f32[512,128]{1,0:T(8,128)S(1)}, f32[512,128]{1,0:T(8,128)S(1)}, u32[]{:S(2)}, u32[]{:S(2)}) collective-permute-start(f32[512,128]{1,0:T(8,128)S(1)} %get-tuple-element.65), channel_id=1, source_target_pairs={{0,16},{16,0},{32,48},{48,32},{64,80},{80,64},{96,112},{112,96},{1... | collective-permute-start | bytes 786440 | tf_op jit(solution)/shard_map/ppermute | solution.py:493
  40.9 23.9 %all-to-all-start.1 = ((f32[256,2,128]{2,1,0:T(2,128)}), f32[256,2,128]{2,1,0:T(2,128)S(1)}, u32[]{:S(2)}, u32[]{:S(2)}) async-start(f32[256,2,128]{2,1,0:T(2,128)} %bitcast.13), calls=%async_computation.1 | async-start | bytes 524288 | tf_op jit(solution)/shard_map/all_to_all | solution.py:553

commit v2 on v1

--- a/solution.py
+++ b/solution.py
@@ -32,14 +32,14 @@
 BUSY = pl.CostEstimate(flops=10**15, bytes_accessed=10**9, transcendentals=0)
 
 
-def call(body, outs, specs, scratch=(), mib=20, cost=None):
+def call(body, outs, specs, scratch=(), mib=20, cost=None, places=None):
     return pl.pallas_call(
         body,
         out_shape=outs,
         in_specs=specs,
-        out_specs=jax.tree.map(lambda _: VMEM, outs),
+        out_specs=places or jax.tree.map(lambda _: VMEM, outs),
         scratch_shapes=list(scratch),
-        compiler_params=pltpu.CompilerParams(vmem_limit_bytes=mib and mib * 1024 * 1024),
+        compiler_params=pltpu.CompilerParams(vmem_limit_bytes=mib * 1024 * 1024),
         cost_estimate=cost,
     )
 
@@ -55,55 +55,50 @@
 
 def pack_windows(plane_ref, out_ref, left, right):
     lane = lanes((8, NZ))
-    sub = lax.broadcasted_iota(jnp.int32, (8, NZ), 0)
-    zero = jnp.zeros((8, NZ), F32)
     for half, side in enumerate((left, right)):
-        side[0:8, :] = zero
-        side[136:144, :] = zero
+        side[0:8, :] = jnp.zeros((8, NZ), F32)
+        side[136:160, :] = jnp.zeros((24, NZ), F32)
         side[8:136, :] = plane_ref[:, NZ * half : NZ * half + NZ]
 
-    def put(block, row, start, at, where=None):
+    def put(block, row, start, at):
         for half, side in enumerate((left, right)):
             lo = max(start, NZ * half)
             hi = min(start + 32, NZ * half + NZ)
-            if lo >= hi:
-                continue
-            here = (lane >= at + lo - start) & (lane < at + hi - start)
-            if where is not None:
-                here = here & where
-            block = jnp.where(here, turn(side[8 + row : 16 + row, :], at - start), block)
+            if lo < hi:
+                here = (lane >= at + lo - start) & (lane < at + hi - start)
+                block = jnp.where(here, turn(side[8 + row : 16 + row, :], at - start), block)
         return block
 
     for chip in range(4):
-        for pair in range(8):
-            rest = zero
-            for odd in range(2):
-                start = 16 * (2 * pair + odd) - 8
-                main = zero
-                for g in range(6):
-                    row = 32 * chip - 8 + 8 * g
-                    if row < 0 or row >= 128:
-                        continue
-                    if g < 4:
-                        main = put(main, row, start, 32 * g)
-                    else:
-                        mine = (sub >= 4) if odd else (sub < 4)
-                        rest = put(rest, row - 4 * odd, start, 32 * (g - 4), mine)
-                        rest = put(rest, row + 4 - 4 * odd, start, 64 + 32 * (g - 4), mine)
-                base = 24 * (8 * chip + pair)
-                out_ref[base + 16 * odd : base + 16 * odd + 8, :] = main
-            out_ref[base + 8 : base + 16, :] = rest
-
-
-def split_windows(arrived, mine, other):
+        for ty in range(16):
+            main = rest = jnp.zeros((8, NZ), F32)
+            for g in range(4):
+                main = put(main, 32 * chip - 6 + 8 * g, 16 * ty - 8, 32 * g)
+                rest = put(rest, 32 * chip + 26 + 3 * g, 16 * ty - 8, 32 * g)
+            row = 11 * (16 * chip + ty)
+            out_ref[row : row + 8, :] = main
+            out_ref[row + 8 : row + 11, :] = rest[0:3]
+
+
+def split_windows(source, mine, other, arrived, sem):
     core = parity()[0] == 1
-    odd = parity()[1]
-    lane = lanes((8, 128))
-    for k in range(64):
-        main = arrived[pl.ds(12 * k + 4 * odd, 8), :]
-        rest = arrived[pl.ds(12 * k + 8 - 8 * odd, 4), :]
-        rest = jnp.concatenate([turn(rest, 64), rest], 0)
-        upper = jnp.where(lane < 64, turn(main, 64), rest)
+    lane = lanes((8, NZ))
+    sub = lax.broadcasted_iota(jnp.int32, (8, NZ), 0)
+    count = mine.shape[0] // 8
+    copy = pltpu.make_async_copy(source.at[pl.ds(0, 11 * count)], arrived.at[pl.ds(0, 11 * count)], sem.at[0])
+    copy.start()
+    arrived[11 * count : 11 * count + 16, :] = jnp.zeros((16, NZ), F32)
+    copy.wait()
+    for k in range(count):
+        row = 11 * k
+
+        def rows(first):
+            return arrived[row + first : row + first + 8, :]
+
+        main = rows(0)
+        third = jnp.where(sub < 3, turn(rows(8), 64), jnp.where(sub < 6, turn(rows(5), 32), rows(2)))
+        fourth = jnp.where(sub < 1, turn(rows(10), 32), jnp.where(sub < 4, rows(7), 0.0))
+        upper = jnp.where(lane < 64, turn(main, 64), jnp.where(lane < 96, third, fourth))
         mine[8 * k : 8 * k + 8, :] = jnp.where(core, upper, main)
         other[8 * k : 8 * k + 8, :] = jnp.where(core, main, upper)
 
@@ -303,8 +298,8 @@
 
 def free(scales, *refs):
     fields, shallow, got, refs = refs[:7], refs[7], refs[8:10], refs[10:]
-    xe, xo, src, SA, CS, BS0, BS1, first, second, IM = refs[:10]
-    U0, U1, C, M0, M1, Q0, Q1, SF, A, US = refs[10:]
+    xe, xo, src, SA, CS, BS0, BS1, first, second, image = refs[:10]
+    U0, U1, C, M0, M1, Q0, Q1, SF, A, US, IM = refs[10:]
     rows = pl.ds(PAD, E)
 
     with jax.named_scope("assemble"):
@@ -378,9 +373,21 @@
         IM[mine] = IM[mine] - A[0, rows, D : D + T, :] * current
 
     loop(D, 4, 4, finish)
-
-
-def meet(SA, CS, BS0, BS1, IM0, mine, got, rec, image, sent, BS, PS, QS, IM):
+    for half in range(2):
+        image[pl.ds(half, 128, stride=2), :] = IM[8 * half : 8 * half + 8].reshape(128, NZ).T
+
+
+def meet(SA, CS, BS0, BS1, free_image, mine, got, rec, image, sent, BS, PS, QS, low, sems):
+    deep = [
+        pltpu.make_async_copy(
+            free_image.at[pl.ds(2 * SH, 256 - 2 * SH)],
+            image.at[pl.ds(256 * shot + 2 * SH, 256 - 2 * SH)],
+            sems.at[shot],
+        )
+        for shot in range(2)
+    ]
+    for copy in deep:
+        copy.start()
     rows = pl.ds(PAD, E)
     with jax.named_scope("turn"):
         core = parity()[0] == 1
@@ -389,9 +396,11 @@
         turned = jnp.concatenate([planes, jnp.zeros((64, NZ), F32)], 0).T
         parts = [turned[32 * g : 32 * g + 32, :] for g in range(4)]
         flat = lanes((E, NZ))
-        PS[0] = turn(parts[0], 64)
-        PS[1] = jnp.where(flat < 64, parts[1], turn(parts[2], 64))
-        PS[2] = parts[3]
+        pairs = [jnp.where(flat < 64, parts[2 * i], turn(parts[2 * i + 1], 64)) for i in range(2)]
+        at = SH * (T - 6)
+        PS[0] = turn(pairs[0], at)
+        PS[1] = jnp.where(flat < at, turn(pairs[0], at), turn(pairs[1], at))
+        PS[2] = turn(pairs[1], at)
 
     with jax.named_scope("shallow"):
         for i in range(STEPS):
@@ -420,13 +429,22 @@
         sent[1] = older[1, H : H + T, :]
 
     with jax.named_scope("image"):
-        here = lanes((T, NZ)) < SH
-        for x in range(T):
-            IM[x] = IM0[x] + jnp.where(here, turn(delta, -SH * x), 0.0)
+        turned = jnp.concatenate([delta, jnp.zeros((NZ - T, NZ), F32)], 0).T
+        lane = lanes((SH, NZ))
         for half in range(2):
-            turned = IM[8 * half : 8 * half + 8].reshape(128, NZ).T
-            for shot in range(2):
-                image[pl.ds(256 * shot + half, 128, stride=2), :] = turned
+            line = jnp.zeros((SH, NZ), F32)
+            for k in range(8):
+                x = 8 * half + k
+                piece = turn(turned[SH * x : SH * x + SH, :], 16 * k)
+                line = jnp.where((lane >= 16 * k) & (lane < 16 * k + 16), piece, line)
+            low[pl.ds(half, SH, stride=2), :] = free_image[pl.ds(half, SH, stride=2), :] + line
+        shallow = [
+            pltpu.make_async_copy(low, image.at[pl.ds(256 * shot, 2 * SH)], sems.at[2 + shot]) for shot in range(2)
+        ]
+        for copy in shallow:
+            copy.start()
+        for copy in (*deep, *shallow):
+            copy.wait()
 
 
 def born(scales, *refs):
@@ -457,7 +475,7 @@
             center, lap = laplace(B.at[t + 1], x, n, PAD, G)
             B[t + 2, rows, ALL_Y, :] = (
                 2.0 * center - B[t, rows, ALL_Y, :] + C[rows, ALL_Y, :] * lap
-                - PT[pl.ds(x - XO + 4, n), 4:28, :] * accel
+                - PT[pl.ds(x - XO + 2, n), 4:28, :] * accel
             )
 
         loop(start, blocks, n, step)
@@ -512,37 +530,48 @@
         [pltpu.SemaphoreType.DMA((8,))],
     )(*[pltpu.with_memory_space_constraint(a, pltpu.HBM) for a in (*fields, perturbation.reshape(128, 256))])
     got = (swap(send_e, "ty", 0), swap(send_o, "ty", 1))
-    side = pltpu.VMEM((144, NZ), F32)
-    blocks = call(pack_windows, shape(768, NZ), [VMEM], [side, side])(plane)
+    side = pltpu.VMEM((160, NZ), F32)
+    blocks = call(pack_windows, shape(704, NZ), [VMEM], [side, side])(plane)
     groups = [[(2 * chip + core) * 16 + ty for chip in range(4) for ty in range(16)] for core in range(2)]
     windows = lax.all_to_all(
-        blocks.reshape(192, 4, NZ), ("tx", "ty"), split_axis=0, concat_axis=0, tiled=True, axis_index_groups=groups
-    ).reshape(768, NZ)
+        blocks.reshape(704, 1, NZ), ("tx", "ty"), split_axis=0, concat_axis=0, tiled=True, axis_index_groups=groups
+    ).reshape(704, NZ)
     pieces = shape(3, E, NZ)
     src, rec, scales = call(count_planes, (pieces, pieces, shape(8, NZ)), [SMEM] + [VMEM] * 5)(
         wavelet, source_x[None], source_y[None], encode_bits, receiver_x[None], receiver_y[None]
     )
-    windows, src, rec, scales = lax.optimization_barrier((windows, src, rec, scales))
-    near, other = call(split_windows, (shape(512, NZ), shape(512, NZ)), [VMEM])(windows)
-    far = swap(other, "tx", 0)
     strip = shape(*STRIP_X)
     send_e, send_o = call(pack_x, (strip, strip), [VMEM] * 10, cost=BUSY)(*fields, shallow, *got)
     across = (swap(send_e, "tx", 0), swap(send_o, "tx", 1))
     one = lambda *dims: pltpu.VMEM(dims, F32)
     cells = shape(*tile)
     low = shape(*LOW)
-    SA, CS, BS0, BS1, first, second, IM = call(
+    SA, CS, BS0, BS1, first, second, image = call(
         free,
-        (shape(STEPS, 3, E, NZ), low, low, low, cells, cells, cells),
+        (shape(STEPS, 3, E, NZ), low, low, low, cells, cells, shape(256, NZ)),
         [VMEM] * 14,
-        [one(*WIDE)] * 7 + [one(*FLAT), one(STEPS, *FLAT), one(2, *LOW)],
+        [one(*WIDE)] * 7 + [one(*FLAT), one(STEPS, *FLAT), one(2, *LOW), one(*tile)],
     )(scales, *fields, shallow, *got, *across, src)
+    sems = lambda n: pltpu.SemaphoreType.DMA((n,))
+
+    def split(windows, count):
+        return call(split_windows, (shape(8 * count, NZ),) * 2, [HBM], [one(11 * count + 16, NZ), sems(1)])(
+            pltpu.with_memory_space_constraint(windows, pltpu.HBM)
+        )
+
+    windows, src = lax.optimization_barrier((windows, src))
+    near, other = split(windows, SH)
+    far = swap(other, "tx", 0)
     image, sent = call(
         meet,
         (shape(512, NZ), shape(2, T, NZ)),
         [VMEM] * 8,
-        [one(4, *LOW), one(3, E, NZ), one(2, *LOW), one(*tile)],
-    )(SA, CS, BS0, BS1, IM, near, far, rec)
+        [one(4, *LOW), one(3, E, NZ), one(2, *LOW), one(2 * SH, NZ), sems(4)],
+        places=(HBM, VMEM),
+    )(SA, CS, BS0, BS1, image, near, far, rec)
+    windows, image = lax.optimization_barrier((windows, image))
+    near, other = split(windows, 64)
+    far = swap(other, "tx", 0)
     last, before, first, second = call(
         born,
         (cells, cells, cells, cells),

time: 66 us -> 65.4 us (level)
  waiting for transfers between devices: 19.2 us -> 15.3 us
  starting transfers between devices: 33 us -> 35.3 us
  Pallas kernels: 12.7 us -> 13.6 us
    all_to_all x1, waiting for transfers between devices: 13.4 us -> 8.69 us  [per_device(): lax.all_to_all(image.reshape(256, 2, NZ), ('shot', 'tx', 'ty'), split_axi...]
    ppermute x5 -> x6, starting transfers between devices: 11.2 us -> 13.2 us  [swap(): return lax.ppermute(cells, axis, pairs)]
    ppermute x5 -> x6, waiting for transfers between devices: 0.01 us -> 1.18 us  [swap(): return lax.ppermute(cells, axis, pairs)]
    pallas_call x3 -> x4, Pallas kernels: 4.36 us -> 5.48 us  [the longest x2 2.23 us: split(): call(split_windows, (shape(8 * count, NZ),) * 2, [HBM], [one(11 * count +...]
  transfers between devices with their start and end apart: 7 -> 8, of which waited for: 2 -> 3; matrix products, arithmetic and copies ran while one was open for 0% -> 0% of each run, Pallas kernels for 13% -> 15%
where the time goes in v2:
time: 65.4 us; the launch traced here: 65 us
  starting transfers between devices  35.3 us (54%)
  waiting for transfers between devices  15.3 us (23%)
  Pallas kernels  13.6 us (21%)
  between operations  0.82 us (1%)
    all_to_all x1, starting transfers between devices, per_device(): lax.all_to_all(blocks.reshape(704, 1, NZ), ('tx', 'ty'), split_axis=0, co...  13.6 us
    ppermute x6, starting transfers between devices, swap(): return lax.ppermute(cells, axis, pairs)  13.2 us
    all_to_all x1, waiting for transfers between devices, per_device(): lax.all_to_all(image.reshape(256, 2, NZ), ('shot', 'tx', 'ty'), split_axi...  8.69 us
    all_to_all x1, starting transfers between devices, per_device(): lax.all_to_all(image.reshape(256, 2, NZ), ('shot', 'tx', 'ty'), split_axi...  8.46 us
    all_to_all x1, waiting for transfers between devices, per_device(): lax.all_to_all(blocks.reshape(704, 1, NZ), ('tx', 'ty'), split_axis=0, co...  5.44 us
    pallas_call x1, Pallas kernels, per_device(): call(born, (cells, cells, cells, cells), [VMEM] * 18, [one(*WIDE)] * 3 +...  2.3 us
    pallas_call x2, Pallas kernels, split(): call(split_windows, (shape(8 * count, NZ),) * 2, [HBM], [one(11 * count +...  2.23 us
    pallas_call x1, Pallas kernels, per_device(): call(free, (shape(STEPS, 3, E, NZ), low, low, low, cells, cells, shape(25...  1.86 us
  transfers between devices with their start and end apart: 8, of which 3 were waited for; matrix products, arithmetic and copies ran while one was open for 0% of the time, Pallas kernels for 15%

profile of v2, /device:TPU:1, one launch (start us, length us, event | category | flops | bytes accessed | tf_op | source)
XLA Modules:
  0.0 65.0 jit_solution(5320339955787352915)
XLA Ops:
  0.6 1.5 %shard_map.173 = (f32[69,8,128]{2,1,0:T(8,128)S(1)}, f32[69,8,128]{2,1,0:T(8,128)S(1)}, f32[80,128]{1,0:T(8,128)S(1)}, f32[16,16,128]{2,1,0:T(8,128)S(1)}, f32[1...) custom-call(f32[16,16,128]{2,1,0:T(8,128)} %bitcast.27, ...), custom_call_target="tpu_custom_call" | custom-call | tf_op jit(solution)/shard_map/pallas_call | solution.py:526
  2.2 2.2 %collective-permute-start = (f32[69,8,128]{2,1,0:T(8,128)S(1)}, f32[69,8,128]{2,1,0:T(8,128)S(1)}, u32[]{:S(2)}, u32[]{:S(2)}) collective-permute-start(f32[69,8,128]{2,1,0:T(8,128)S(1)} %get-tuple-element.54), channel_id=1, source_target_pairs={{0,1},{1,0},{2,3},{3,2},{4,5},{5,4},{6,7},{7,6},{8,9},{9,8},{10,11... | collective-permute-start | bytes 847880 | tf_op jit(solution)/shard_map/ppermute | solution.py:511
  4.4 0.7 %collective-permute-start.1 = (f32[69,8,128]{2,1,0:T(8,128)S(1)}, f32[69,8,128]{2,1,0:T(8,128)S(1)}, u32[]{:S(2)}, u32[]{:S(2)}) collective-permute-start(f32[69,8,128]{2,1,0:T(8,128)S(1)} %get-tuple-element.55), channel_id=1, source_target_pairs={{1,2},{2,1},{3,4},{4,3},{5,6},{6,5},{7,8},{8,7},{9,10},{10,9},{11,... | collective-permute-start | bytes 847880 | tf_op jit(solution)/shard_map/ppermute | solution.py:511
  5.1 1.4 %shard_map.174 = f32[704,128]{1,0:T(8,128)} custom-call(f32[128,256]{1,0:T(8,128)S(1)} %get-tuple-element.42.plane_ref), custom_call_target="tpu_custom_call" | custom-call | tf_op jit(solution)/shard_map/pallas_call | solution.py:534
  6.5 13.6 %all-to-all-start = ((f32[704,1,128]{2,1,0:T(1,128)}), f32[704,1,128]{2,1,0:T(1,128)}, u32[]{:S(2)}, u32[]{:S(2)}) async-start(f32[704,1,128]{2,1,0:T(1,128)} %bitcast.8), calls=%async_computation | async-start | bytes 720896 | tf_op jit(solution)/shard_map/all_to_all | solution.py:536
  20.1 0.0 collective-permute-done.refs_8_.refs_7_
  20.1 0.0 collective-permute-done.1.refs_9_.refs_8_
  20.1 0.0 copy-start
  20.1 0.0 copy-start.1
  20.1 0.0 copy-start.2
  20.1 0.0 copy-start.3
  20.1 0.0 copy-start.4
  20.1 0.0 copy-start.5
  20.1 0.8 %shard_map.176 = (f32[760,128]{1,0:T(8,128)}, f32[760,128]{1,0:T(8,128)S(1)}) custom-call(f32[16,16,128]{2,1,0:T(8,128)S(1)} %get-tuple-element.46.refs_0_, f32[16,16,128]{2,1,0:T(8,128)S(1)} %get-tuple-element.47.refs_1_, f32[16,16,128]{2,1,0:T(8,128)S(1)} %get-tuple-element.48.refs_2_, f32[16,16,128]{2,1,0:T(8,128)S(1)} %get-tuple-element.49.refs_3_, ...), custom_call_target="tpu_custom_call" | custom-call | flops 999999986991104 | bytes 1000000000 | tf_op jit(solution)/shard_map/pallas_call | solution.py:544
  21.0 1.5 %collective-permute-start.2 = (f32[760,128]{1,0:T(8,128)}, f32[760,128]{1,0:T(8,128)S(1)}, u32[]{:S(2)}, u32[]{:S(2)}) collective-permute-start(f32[760,128]{1,0:T(8,128)} %get-tuple-element.56), channel_id=1, source_target_pairs={{0,16},{16,0},{32,48},{48,32},{64,80},{80,64},{96,112},{112,96},{1... | collective-permute-start | bytes 1167368 | tf_op jit(solution)/shard_map/ppermute | solution.py:511
  22.5 3.0 %collective-permute-start.3 = (f32[760,128]{1,0:T(8,128)S(1)}, f32[760,128]{1,0:T(8,128)S(1)}, u32[]{:S(2)}, u32[]{:S(2)}) collective-permute-start(f32[760,128]{1,0:T(8,128)S(1)} %get-tuple-element.57), channel_id=1, source_target_pairs={{16,32},{32,16},{48,64},{64,48},{80,96},{96,80},{17,33},{33,17},{4... | collective-permute-start | bytes 1167368 | tf_op jit(solution)/shard_map/ppermute | solution.py:511
  25.6 1.0 %shard_map.175 = (f32[3,32,128]{2,1,0:T(8,128)S(1)}, f32[3,32,128]{2,1,0:T(8,128)S(1)}, f32[8,128]{1,0:T(8,128)S(1)}) custom-call(f32[4]{0:T(128)S(1)} %copy-done.5, s32[1,256]{1,0:T(1,128)S(1)} %bitcast.25, s32[1,256]{1,0:T(1,128)S(1)} %bitcast.26, s32[1,256]{1,0:T(1,128)S(1)} %copy-done.4, s32[1,1024]{1,0:T(1,128)S(1)} %bitcast.23, s32[1,1024]{1,0:T(1,128)S(1)} %bitcast.24), custom_call_target="tpu_custom_call" | custom-call | tf_op jit(solution)/shard_map/pallas_call | solution.py:540
  26.6 5.4 %all-to-all-done = f32[704,1,128]{2,1,0:T(1,128)} async-done(((f32[704,1,128]{2,1,0:T(1,128)}), f32[704,1,128]{2,1,0:T(1,128)}, u32[]{:S(2)}, u32[]{:S(2)}) %all-to-all-start) | async-done | bytes 360480 | tf_op jit(solution)/shard_map/all_to_all | solution.py:536
  32.0 0.9 %shard_map.178 = (f32[64,128]{1,0:T(8,128)S(1)}, f32[64,128]{1,0:T(8,128)S(1)}) custom-call(f32[704,128]{1,0:T(8,128)} %bitcast.9.source), custom_call_target="tpu_custom_call" | custom-call | tf_op jit(solution)/shard_map/pallas_call | solution.py:558
  32.9 3.6 %collective-permute-start.4 = (f32[64,128]{1,0:T(8,128)S(1)}, f32[64,128]{1,0:T(8,128)S(1)}, u32[]{:S(2)}, u32[]{:S(2)}) collective-permute-start(f32[64,128]{1,0:T(8,128)S(1)} %get-tuple-element.64), channel_id=1, source_target_pairs={{0,16},{16,0},{32,48},{48,32},{64,80},{80,64},{96,112},{112,96},{1... | collective-permute-start | bytes 98312 | tf_op jit(solution)/shard_map/ppermute | solution.py:511
  36.5 0.0 collective-permute-done.2.refs_10_.refs_9_
  36.5 0.0 collective-permute-done.3.refs_11_.refs_10_
  36.5 1.9 %shard_map.177 = (f32[4,3,32,128]{3,2,1,0:T(8,128)S(1)}, f32[3,48,128]{2,1,0:T(8,128)S(1)}, f32[3,48,128]{2,1,0:T(8,128)S(1)}, f32[3,48,128]{2,1,0:T(8,128)S(1)}...) custom-call(f32[8,128]{1,0:T(8,128)S(1)} %get-tuple-element.45.scales, ...), custom_call_target="tpu_custom_call" | custom-call | tf_op jit(solution)/shard_map/pallas_call | solution.py:549
  38.4 0.0 collective-permute-done.4.got
  38.4 1.6 %shard_map.179 = (f32[512,128]{1,0:T(8,128)}, f32[2,16,128]{2,1,0:T(8,128)S(1)}) custom-call(f32[4,3,32,128]{3,2,1,0:T(8,128)S(1)} %get-tuple-element.58.SA, f32[3,48,128]{2,1,0:T(8,128)S(1)} %get-tuple-element.59.CS, f32[3,48,128]{2,1,0:T(8,128)S(1)} %get-tuple-element.60.BS0, f32[3,48,128]{2,1,0:T(8,128)S(1)} %get-tuple-element.61.BS1, ...), custom_call_target="tpu_custom_call" | custom-call | tf_op jit(solution)/shard_map/pallas_call | solution.py:565
  40.0 8.5 %all-to-all-start.1 = ((f32[256,2,128]{2,1,0:T(2,128)}), f32[256,2,128]{2,1,0:T(2,128)S(1)}, u32[]{:S(2)}, u32[]{:S(2)}) async-start(f32[256,2,128]{2,1,0:T(2,128)} %bitcast.14), calls=%async_computation.1 | async-start | bytes 524288 | tf_op jit(solution)/shard_map/all_to_all | solution.py:582
  48.5 1.3 %shard_map.181 = (f32[512,128]{1,0:T(8,128)S(1)}, f32[512,128]{1,0:T(8,128)S(1)}) custom-call(f32[704,128]{1,0:T(8,128)} %bitcast.9.source), custom_call_target="tpu_custom_call" | custom-call | tf_op jit(solution)/shard_map/pallas_call | solution.py:558
  49.8 2.2 %collective-permute-start.5 = (f32[512,128]{1,0:T(8,128)S(1)}, f32[512,128]{1,0:T(8,128)S(1)}, u32[]{:S(2)}, u32[]{:S(2)}) collective-permute-start(f32[512,128]{1,0:T(8,128)S(1)} %get-tuple-element.71), channel_id=1, source_target_pairs={{0,16},{16,0},{32,48},{48,32},{64,80},{80,64},{96,112},{112,96},{1... | collective-permute-start | bytes 786440 | tf_op jit(solution)/shard_map/ppermute | solution.py:511
  52.1 1.2 %collective-permute-done.5.refs_13_ = f32[512,128]{1,0:T(8,128)S(1)} collective-permute-done((f32[512,128]{1,0:T(8,128)S(1)}, f32[512,128]{1,0:T(8,128)S(1)}, u32[]{:S(2)}, u32[]{:S(2)}) %collective-permute-start.5) | collective-permute-done | bytes 262176 | tf_op jit(solution)/shard_map/ppermute | solution.py:511
  53.2 2.3 %shard_map.182 = (f32[16,16,128]{2,1,0:T(8,128)}, f32[16,16,128]{2,1,0:T(8,128)}, f32[16,16,128]{2,1,0:T(8,128)}, f32[16,16,128]{2,1,0:T(8,128)}) custom-call(f32[8,128]{1,0:T(8,128)S(1)} %get-tuple-element.45.scales, f32[16,16,128]{2,1,0:T(8,128)S(1)} %get-tuple-element.46.refs_0_, f32[16,16,128]{2,1,0:T(8,128)S(1)} %get-tuple-element.47.refs_1_, ...), custom_call_target="tpu_custom_call" | custom-call | tf_op jit(solution)/shard_map/pallas_call | solution.py:575
  55.5 8.7 %all-to-all-done.1 = f32[256,2,128]{2,1,0:T(2,128)S(1)} async-done(((f32[256,2,128]{2,1,0:T(2,128)}), f32[256,2,128]{2,1,0:T(2,128)S(1)}, u32[]{:S(2)}, u32[]{:S(2)}) %all-to-all-start.1) | async-done | bytes 262176 | tf_op jit(solution)/shard_map/all_to_all | solution.py:582
  64.2 0.8 %shard_map.180 = f32[128,128]{1,0:T(8,128)} custom-call(f32[512,128]{1,0:T(8,128)S(1)} %bitcast.22), custom_call_target="tpu_custom_call" | custom-call | tf_op jit(solution)/shard_map/pallas_call | solution.py:585
  (6 shorter events, 0.0 us)
Async XLA Ops:
  2.2 17.9 %collective-permute-start = (f32[69,8,128]{2,1,0:T(8,128)S(1)}, f32[69,8,128]{2,1,0:T(8,128)S(1)}, u32[]{:S(2)}, u32[]{:S(2)}) collective-permute-start(f32[69,8,128]{2,1,0:T(8,128)S(1)} %get-tuple-element.54), channel_id=1, source_target_pairs={{0,1},{1,0},{2,3},{3,2},{4,5},{5,4},{6,7},{7,6},{8,9},{9,8},{10,11... | collective-permute-start | bytes 847880 | tf_op jit(solution)/shard_map/ppermute | solution.py:511
  4.4 15.7 %collective-permute-start.1 = (f32[69,8,128]{2,1,0:T(8,128)S(1)}, f32[69,8,128]{2,1,0:T(8,128)S(1)}, u32[]{:S(2)}, u32[]{:S(2)}) collective-permute-start(f32[69,8,128]{2,1,0:T(8,128)S(1)} %get-tuple-element.55), channel_id=1, source_target_pairs={{1,2},{2,1},{3,4},{4,3},{5,6},{6,5},{7,8},{8,7},{9,10},{10,9},{11,... | collective-permute-start | bytes 847880 | tf_op jit(solution)/shard_map/ppermute | solution.py:511
  6.5 25.5 %all-to-all-start = ((f32[704,1,128]{2,1,0:T(1,128)}), f32[704,1,128]{2,1,0:T(1,128)}, u32[]{:S(2)}, u32[]{:S(2)}) async-start(f32[704,1,128]{2,1,0:T(1,128)} %bitcast.8), calls=%async_computation | async-start | bytes 720896 | tf_op jit(solution)/shard_map/all_to_all | solution.py:536
  20.1 5.5 %copy-start = (s32[1024]{0:T(1024)S(1)}, s32[1024]{0:T(1024)}, u32[]{:S(2)}) copy-start(s32[1024]{0:T(1024)} %param.26) | copy-start | bytes 12292
  20.1 5.5 %copy-start.1 = (s32[1024]{0:T(1024)S(1)}, s32[1024]{0:T(1024)}, u32[]{:S(2)}) copy-start(s32[1024]{0:T(1024)} %param.27) | copy-start | bytes 12292
  20.1 5.5 %copy-start.2 = (s32[256]{0:T(256)S(1)}, s32[256]{0:T(256)}, u32[]{:S(2)}) copy-start(s32[256]{0:T(256)} %param.24) | copy-start | bytes 3076
  20.1 5.5 %copy-start.3 = (s32[256]{0:T(256)S(1)}, s32[256]{0:T(256)}, u32[]{:S(2)}) copy-start(s32[256]{0:T(256)} %param.25) | copy-start | bytes 3076
  20.1 5.5 %copy-start.4 = (s32[1,256]{1,0:T(1,128)S(1)}, s32[1,256]{1,0:T(1,128)}, u32[]{:S(2)}) copy-start(s32[1,256]{1,0:T(1,128)} %bits.1) | copy-start | bytes 3076
  20.1 5.5 %copy-start.5 = (f32[4]{0:T(128)S(1)}, f32[4]{0:T(128)}, u32[]{:S(2)}) copy-start(f32[4]{0:T(128)} %wavelet.1) | copy-start | bytes 52
  21.0 15.5 %collective-permute-start.2 = (f32[760,128]{1,0:T(8,128)}, f32[760,128]{1,0:T(8,128)S(1)}, u32[]{:S(2)}, u32[]{:S(2)}) collective-permute-start(f32[760,128]{1,0:T(8,128)} %get-tuple-element.56), channel_id=1, source_target_pairs={{0,16},{16,0},{32,48},{48,32},{64,80},{80,64},{96,112},{112,96},{1... | collective-permute-start | bytes 1167368 | tf_op jit(solution)/shard_map/ppermute | solution.py:511
  22.5 14.0 %collective-permute-start.3 = (f32[760,128]{1,0:T(8,128)S(1)}, f32[760,128]{1,0:T(8,128)S(1)}, u32[]{:S(2)}, u32[]{:S(2)}) collective-permute-start(f32[760,128]{1,0:T(8,128)S(1)} %get-tuple-element.57), channel_id=1, source_target_pairs={{16,32},{32,16},{48,64},{64,48},{80,96},{96,80},{17,33},{33,17},{4... | collective-permute-start | bytes 1167368 | tf_op jit(solution)/shard_map/ppermute | solution.py:511
  32.9 5.5 %collective-permute-start.4 = (f32[64,128]{1,0:T(8,128)S(1)}, f32[64,128]{1,0:T(8,128)S(1)}, u32[]{:S(2)}, u32[]{:S(2)}) collective-permute-start(f32[64,128]{1,0:T(8,128)S(1)} %get-tuple-element.64), channel_id=1, source_target_pairs={{0,16},{16,0},{32,48},{48,32},{64,80},{80,64},{96,112},{112,96},{1... | collective-permute-start | bytes 98312 | tf_op jit(solution)/shard_map/ppermute | solution.py:511
  40.0 24.2 %all-to-all-start.1 = ((f32[256,2,128]{2,1,0:T(2,128)}), f32[256,2,128]{2,1,0:T(2,128)S(1)}, u32[]{:S(2)}, u32[]{:S(2)}) async-start(f32[256,2,128]{2,1,0:T(2,128)} %bitcast.14), calls=%async_computation.1 | async-start | bytes 524288 | tf_op jit(solution)/shard_map/all_to_all | solution.py:582
  49.8 3.4 %collective-permute-start.5 = (f32[512,128]{1,0:T(8,128)S(1)}, f32[512,128]{1,0:T(8,128)S(1)}, u32[]{:S(2)}, u32[]{:S(2)}) collective-permute-start(f32[512,128]{1,0:T(8,128)S(1)} %get-tuple-element.71), channel_id=1, source_target_pairs={{0,16},{16,0},{32,48},{48,32},{64,80},{80,64},{96,112},{112,96},{1... | collective-permute-start | bytes 786440 | tf_op jit(solution)/shard_map/ppermute | solution.py:511

commit v3 on v2

--- a/solution.py
+++ b/solution.py
@@ -18,9 +18,13 @@
 XO = 1
 SH = 8
 WIDTHS = (4, 4, 4, 4, 3, 3, 3)
-OFFSETS = tuple(sum(WIDTHS[:i]) * G for i in range(len(WIDTHS)))
+LENGTHS = tuple(tuple(T + 2 * (w - 1 - q) for q in range(w)) for w in WIDTHS)
+OFFSETS = tuple(
+    tuple(sum(map(sum, LENGTHS[:f])) + sum(lengths[:q]) for q in range(len(lengths)))
+    for f, lengths in enumerate(LENGTHS)
+)
 SHALLOW = (0, 1, 2, 4, 5)
-SHALLOW_ROW = sum(WIDTHS) * G
+SHALLOW_ROW = -(-sum(map(sum, LENGTHS)) // 8) * 8
 STRIP_Y = (4 * T + 5, 8, NZ)
 STRIP_X = (SHALLOW_ROW + len(SHALLOW) * E, NZ)
 F32 = jnp.float32
@@ -162,14 +166,14 @@
     for f, ref in enumerate(fields):
         width = WIDTHS[f]
         for low, out in ((odd_x, e_ref), (1 - odd_x, o_ref)):
-            first = (1 - low) * (T - width)
-            for i in range(width):
-                x = first + i
-                row = OFFSETS[f] + G * i
-                below, above = beside_y(got, f, lambda start: start + x)
-                out[row : row + 4, :] = below
-                out[row + 4 : row + 20, :] = ref[x]
-                out[row + 20 : row + 24, :] = above
+            for q in range(width):
+                x = low * q + (1 - low) * (T - 1 - q)
+                row, more = OFFSETS[f][q], width - 1 - q
+                if more:
+                    below, above = beside_y(got, f, lambda start: start + x)
+                    out[row : row + more, :] = below[4 - more : 4]
+                    out[row + more + T : row + more + T + more, :] = above[0:more]
+                out[row + more : row + more + T, :] = ref[x]
     for i in range(len(SHALLOW)):
         row = SHALLOW_ROW + E * i
         below, above = shallow_beside_y(got, i)
@@ -219,11 +223,12 @@
 
 def shallow_laplace(ref):
     rows = pl.ds(PAD, E)
-    lane = lanes((3, E, NZ))
+    lane = lanes((1, 1, NZ))
+    depth = lane & (SH - 1)
     center = ref[:, rows, :]
     total = ref[:, pl.ds(PAD + 1, E), :] + ref[:, pl.ds(PAD - 1, E), :]
-    total = total + jnp.where(lane % SH == SH - 1, 0.0, turn(center, -1))
-    total = total + jnp.where(lane % SH == 0, 0.0, turn(center, 1))
+    total = total + jnp.where(depth == SH - 1, 0.0, turn(center, -1))
+    total = total + jnp.where(depth == 0, 0.0, turn(center, 1))
     left = turn(center, SH)
     right = turn(center, -SH)
     none = jnp.zeros((1, E, NZ), F32)
@@ -258,13 +263,13 @@
     below, above = beside_y(got, f, lambda start: slice(start, start + T))
     ext[OWN_X, PAD : PAD + 4, :] = below
     ext[OWN_X, PAD + 20 : PAD + 24, :] = above
-    width = WIDTHS[f]
-    for i in range(width):
-        rows = pl.ds(OFFSETS[f] + G * i, G)
+    for q, length in enumerate(LENGTHS[f]):
+        rows = pl.ds(OFFSETS[f][q], length)
+        at = pl.ds(PAD + D - (length - T) // 2, length)
         got_e = xe[rows, :]
         got_o = xo[rows, :]
-        ext[XO + D - width + i, ALL_Y, :] = jnp.where(odd, got_e, got_o)
-        ext[XO + D + T + i, ALL_Y, :] = jnp.where(odd, got_o, got_e)
+        ext[XO + D - 1 - q, at, :] = jnp.where(odd, got_e, got_o)
+        ext[XO + D + T + q, at, :] = jnp.where(odd, got_o, got_e)
 
 
 def assemble_shallow(i, mine, ext, got, xe, xo):

time: 65.4 us -> 64.9 us (level)
  Pallas kernels: 13.6 us -> 12.8 us
  waiting for transfers between devices: 15.3 us -> 16 us
    pallas_call x1, Pallas kernels: 0.85 us -> 0.08 us  [per_device(): call(pack_x, (strip, strip), [VMEM] * 10, cost=BUSY)(*fields, shallow, *got)]
    all_to_all x1, waiting for transfers between devices: 5.44 us -> 6.09 us  [per_device(): lax.all_to_all(blocks.reshape(704, 1, NZ), ('tx', 'ty'), split_axis=0, co...]
  transfers between devices with their start and end apart: 8 -> 8, of which waited for: 3 -> 3; matrix products, arithmetic and copies ran while one was open for 0% -> 0% of each run, Pallas kernels for 15% -> 14%
where the time goes in v3:
time: 64.9 us; the launch traced here: 64.5 us
  starting transfers between devices  34.9 us (54%)
  waiting for transfers between devices  16 us (25%)
  Pallas kernels  12.8 us (20%)
  between operations  0.83 us (1%)
    all_to_all x1, starting transfers between devices, per_device(): lax.all_to_all(blocks.reshape(704, 1, NZ), ('tx', 'ty'), split_axis=0, co...  13.6 us
    ppermute x6, starting transfers between devices, swap(): return lax.ppermute(cells, axis, pairs)  13.4 us
    all_to_all x1, waiting for transfers between devices, per_device(): lax.all_to_all(image.reshape(256, 2, NZ), ('shot', 'tx', 'ty'), split_axi...  8.69 us
    all_to_all x1, starting transfers between devices, per_device(): lax.all_to_all(image.reshape(256, 2, NZ), ('shot', 'tx', 'ty'), split_axi...  7.92 us
    all_to_all x1, waiting for transfers between devices, per_device(): lax.all_to_all(blocks.reshape(704, 1, NZ), ('tx', 'ty'), split_axis=0, co...  6.09 us
    pallas_call x1, Pallas kernels, per_device(): call(born, (cells, cells, cells, cells), [VMEM] * 18, [one(*WIDE)] * 3 +...  2.3 us
    pallas_call x2, Pallas kernels, split(): call(split_windows, (shape(8 * count, NZ),) * 2, [HBM], [one(11 * count +...  2.23 us
    pallas_call x1, Pallas kernels, per_device(): call(free, (shape(STEPS, 3, E, NZ), low, low, low, cells, cells, shape(25...  1.86 us
  transfers between devices with their start and end apart: 8, of which 3 were waited for; matrix products, arithmetic and copies ran while one was open for 0% of the time, Pallas kernels for 14%

profile of v3, /device:TPU:1, one launch (start us, length us, event | category | flops | bytes accessed | tf_op | source)
XLA Modules:
  0.0 64.5 jit_solution(17900208386725930388)
XLA Ops:
  0.6 1.5 %shard_map.173 = (f32[69,8,128]{2,1,0:T(8,128)S(1)}, f32[69,8,128]{2,1,0:T(8,128)S(1)}, f32[80,128]{1,0:T(8,128)S(1)}, f32[16,16,128]{2,1,0:T(8,128)S(1)}, f32[1...) custom-call(f32[16,16,128]{2,1,0:T(8,128)} %bitcast.27, ...), custom_call_target="tpu_custom_call" | custom-call | tf_op jit(solution)/shard_map/pallas_call | solution.py:531
  2.2 2.2 %collective-permute-start = (f32[69,8,128]{2,1,0:T(8,128)S(1)}, f32[69,8,128]{2,1,0:T(8,128)S(1)}, u32[]{:S(2)}, u32[]{:S(2)}) collective-permute-start(f32[69,8,128]{2,1,0:T(8,128)S(1)} %get-tuple-element.54), channel_id=1, source_target_pairs={{0,1},{1,0},{2,3},{3,2},{4,5},{5,4},{6,7},{7,6},{8,9},{9,8},{10,11... | collective-permute-start | bytes 847880 | tf_op jit(solution)/shard_map/ppermute | solution.py:516
  4.4 0.7 %collective-permute-start.1 = (f32[69,8,128]{2,1,0:T(8,128)S(1)}, f32[69,8,128]{2,1,0:T(8,128)S(1)}, u32[]{:S(2)}, u32[]{:S(2)}) collective-permute-start(f32[69,8,128]{2,1,0:T(8,128)S(1)} %get-tuple-element.55), channel_id=1, source_target_pairs={{1,2},{2,1},{3,4},{4,3},{5,6},{6,5},{7,8},{8,7},{9,10},{10,9},{11,... | collective-permute-start | bytes 847880 | tf_op jit(solution)/shard_map/ppermute | solution.py:516
  5.1 1.4 %shard_map.174 = f32[704,128]{1,0:T(8,128)} custom-call(f32[128,256]{1,0:T(8,128)S(1)} %get-tuple-element.42.plane_ref), custom_call_target="tpu_custom_call" | custom-call | tf_op jit(solution)/shard_map/pallas_call | solution.py:539
  6.5 13.6 %all-to-all-start = ((f32[704,1,128]{2,1,0:T(1,128)}), f32[704,1,128]{2,1,0:T(1,128)}, u32[]{:S(2)}, u32[]{:S(2)}) async-start(f32[704,1,128]{2,1,0:T(1,128)} %bitcast.8), calls=%async_computation | async-start | bytes 720896 | tf_op jit(solution)/shard_map/all_to_all | solution.py:541
  20.1 0.0 collective-permute-done.refs_8_.refs_7_
  20.1 0.0 collective-permute-done.1.refs_9_.refs_8_
  20.1 0.0 copy-start
  20.1 0.0 copy-start.1
  20.1 0.0 copy-start.2
  20.1 0.0 copy-start.3
  20.1 0.0 copy-start.4
  20.1 0.0 copy-start.5
  20.1 0.1 shard_map.176
  20.2 1.6 %collective-permute-start.2 = (f32[632,128]{1,0:T(8,128)S(1)}, f32[632,128]{1,0:T(8,128)S(1)}, u32[]{:S(2)}, u32[]{:S(2)}) collective-permute-start(f32[632,128]{1,0:T(8,128)S(1)} %get-tuple-element.56), channel_id=1, source_target_pairs={{0,16},{16,0},{32,48},{48,32},{64,80},{80,64},{96,112},{112,96},{1... | collective-permute-start | bytes 970760 | tf_op jit(solution)/shard_map/ppermute | solution.py:516
  21.8 3.0 %collective-permute-start.3 = (f32[632,128]{1,0:T(8,128)S(1)}, f32[632,128]{1,0:T(8,128)S(1)}, u32[]{:S(2)}, u32[]{:S(2)}) collective-permute-start(f32[632,128]{1,0:T(8,128)S(1)} %get-tuple-element.57), channel_id=1, source_target_pairs={{16,32},{32,16},{48,64},{64,48},{80,96},{96,80},{17,33},{33,17},{4... | collective-permute-start | bytes 970760 | tf_op jit(solution)/shard_map/ppermute | solution.py:516
  24.9 1.0 %shard_map.175 = (f32[3,32,128]{2,1,0:T(8,128)S(1)}, f32[3,32,128]{2,1,0:T(8,128)S(1)}, f32[8,128]{1,0:T(8,128)S(1)}) custom-call(f32[4]{0:T(128)S(1)} %copy-done.5, s32[1,256]{1,0:T(1,128)S(1)} %bitcast.25, s32[1,256]{1,0:T(1,128)S(1)} %bitcast.26, s32[1,256]{1,0:T(1,128)S(1)} %copy-done.4, s32[1,1024]{1,0:T(1,128)S(1)} %bitcast.23, s32[1,1024]{1,0:T(1,128)S(1)} %bitcast.24), custom_call_target="tpu_custom_call" | custom-call | tf_op jit(solution)/shard_map/pallas_call | solution.py:545
  25.9 6.1 %all-to-all-done = f32[704,1,128]{2,1,0:T(1,128)} async-done(((f32[704,1,128]{2,1,0:T(1,128)}), f32[704,1,128]{2,1,0:T(1,128)}, u32[]{:S(2)}, u32[]{:S(2)}) %all-to-all-start) | async-done | bytes 360480 | tf_op jit(solution)/shard_map/all_to_all | solution.py:541
  32.0 0.9 %shard_map.178 = (f32[64,128]{1,0:T(8,128)S(1)}, f32[64,128]{1,0:T(8,128)S(1)}) custom-call(f32[704,128]{1,0:T(8,128)} %bitcast.9.source), custom_call_target="tpu_custom_call" | custom-call | tf_op jit(solution)/shard_map/pallas_call | solution.py:563
  32.9 3.6 %collective-permute-start.4 = (f32[64,128]{1,0:T(8,128)S(1)}, f32[64,128]{1,0:T(8,128)S(1)}, u32[]{:S(2)}, u32[]{:S(2)}) collective-permute-start(f32[64,128]{1,0:T(8,128)S(1)} %get-tuple-element.64), channel_id=1, source_target_pairs={{0,16},{16,0},{32,48},{48,32},{64,80},{80,64},{96,112},{112,96},{1... | collective-permute-start | bytes 98312 | tf_op jit(solution)/shard_map/ppermute | solution.py:516
  36.5 0.0 collective-permute-done.2.refs_10_.refs_9_
  36.5 0.0 collective-permute-done.3.refs_11_.refs_10_
  36.5 1.9 %shard_map.177 = (f32[4,3,32,128]{3,2,1,0:T(8,128)S(1)}, f32[3,48,128]{2,1,0:T(8,128)S(1)}, f32[3,48,128]{2,1,0:T(8,128)S(1)}, f32[3,48,128]{2,1,0:T(8,128)S(1)}...) custom-call(f32[8,128]{1,0:T(8,128)S(1)} %get-tuple-element.45.scales, ...), custom_call_target="tpu_custom_call" | custom-call | tf_op jit(solution)/shard_map/pallas_call | solution.py:554
  38.4 0.0 collective-permute-done.4.got
  38.4 1.6 %shard_map.179 = (f32[512,128]{1,0:T(8,128)}, f32[2,16,128]{2,1,0:T(8,128)S(1)}) custom-call(f32[4,3,32,128]{3,2,1,0:T(8,128)S(1)} %get-tuple-element.58.SA, f32[3,48,128]{2,1,0:T(8,128)S(1)} %get-tuple-element.59.CS, f32[3,48,128]{2,1,0:T(8,128)S(1)} %get-tuple-element.60.BS0, f32[3,48,128]{2,1,0:T(8,128)S(1)} %get-tuple-element.61.BS1, ...), custom_call_target="tpu_custom_call" | custom-call | tf_op jit(solution)/shard_map/pallas_call | solution.py:570
  40.0 7.9 %all-to-all-start.1 = ((f32[256,2,128]{2,1,0:T(2,128)}), f32[256,2,128]{2,1,0:T(2,128)S(1)}, u32[]{:S(2)}, u32[]{:S(2)}) async-start(f32[256,2,128]{2,1,0:T(2,128)} %bitcast.14), calls=%async_computation.1 | async-start | bytes 524288 | tf_op jit(solution)/shard_map/all_to_all | solution.py:587
  47.9 1.3 %shard_map.181 = (f32[512,128]{1,0:T(8,128)S(1)}, f32[512,128]{1,0:T(8,128)S(1)}) custom-call(f32[704,128]{1,0:T(8,128)} %bitcast.9.source), custom_call_target="tpu_custom_call" | custom-call | tf_op jit(solution)/shard_map/pallas_call | solution.py:563
  49.3 2.2 %collective-permute-start.5 = (f32[512,128]{1,0:T(8,128)S(1)}, f32[512,128]{1,0:T(8,128)S(1)}, u32[]{:S(2)}, u32[]{:S(2)}) collective-permute-start(f32[512,128]{1,0:T(8,128)S(1)} %get-tuple-element.71), channel_id=1, source_target_pairs={{0,16},{16,0},{32,48},{48,32},{64,80},{80,64},{96,112},{112,96},{1... | collective-permute-start | bytes 786440 | tf_op jit(solution)/shard_map/ppermute | solution.py:516
  51.5 1.2 %collective-permute-done.5.refs_13_ = f32[512,128]{1,0:T(8,128)S(1)} collective-permute-done((f32[512,128]{1,0:T(8,128)S(1)}, f32[512,128]{1,0:T(8,128)S(1)}, u32[]{:S(2)}, u32[]{:S(2)}) %collective-permute-start.5) | collective-permute-done | bytes 262176 | tf_op jit(solution)/shard_map/ppermute | solution.py:516
  52.7 2.3 %shard_map.182 = (f32[16,16,128]{2,1,0:T(8,128)}, f32[16,16,128]{2,1,0:T(8,128)}, f32[16,16,128]{2,1,0:T(8,128)}, f32[16,16,128]{2,1,0:T(8,128)}) custom-call(f32[8,128]{1,0:T(8,128)S(1)} %get-tuple-element.45.scales, f32[16,16,128]{2,1,0:T(8,128)S(1)} %get-tuple-element.46.refs_0_, f32[16,16,128]{2,1,0:T(8,128)S(1)} %get-tuple-element.47.refs_1_, ...), custom_call_target="tpu_custom_call" | custom-call | tf_op jit(solution)/shard_map/pallas_call | solution.py:580
  55.0 8.7 %all-to-all-done.1 = f32[256,2,128]{2,1,0:T(2,128)S(1)} async-done(((f32[256,2,128]{2,1,0:T(2,128)}), f32[256,2,128]{2,1,0:T(2,128)S(1)}, u32[]{:S(2)}, u32[]{:S(2)}) %all-to-all-start.1) | async-done | bytes 262176 | tf_op jit(solution)/shard_map/all_to_all | solution.py:587
  63.7 0.8 %shard_map.180 = f32[128,128]{1,0:T(8,128)} custom-call(f32[512,128]{1,0:T(8,128)S(1)} %bitcast.22), custom_call_target="tpu_custom_call" | custom-call | tf_op jit(solution)/shard_map/pallas_call | solution.py:590
  (6 shorter events, 0.0 us)
Async XLA Ops:
  2.2 17.9 %collective-permute-start = (f32[69,8,128]{2,1,0:T(8,128)S(1)}, f32[69,8,128]{2,1,0:T(8,128)S(1)}, u32[]{:S(2)}, u32[]{:S(2)}) collective-permute-start(f32[69,8,128]{2,1,0:T(8,128)S(1)} %get-tuple-element.54), channel_id=1, source_target_pairs={{0,1},{1,0},{2,3},{3,2},{4,5},{5,4},{6,7},{7,6},{8,9},{9,8},{10,11... | collective-permute-start | bytes 847880 | tf_op jit(solution)/shard_map/ppermute | solution.py:516
  4.4 15.7 %collective-permute-start.1 = (f32[69,8,128]{2,1,0:T(8,128)S(1)}, f32[69,8,128]{2,1,0:T(8,128)S(1)}, u32[]{:S(2)}, u32[]{:S(2)}) collective-permute-start(f32[69,8,128]{2,1,0:T(8,128)S(1)} %get-tuple-element.55), channel_id=1, source_target_pairs={{1,2},{2,1},{3,4},{4,3},{5,6},{6,5},{7,8},{8,7},{9,10},{10,9},{11,... | collective-permute-start | bytes 847880 | tf_op jit(solution)/shard_map/ppermute | solution.py:516
  6.5 25.5 %all-to-all-start = ((f32[704,1,128]{2,1,0:T(1,128)}), f32[704,1,128]{2,1,0:T(1,128)}, u32[]{:S(2)}, u32[]{:S(2)}) async-start(f32[704,1,128]{2,1,0:T(1,128)} %bitcast.8), calls=%async_computation | async-start | bytes 720896 | tf_op jit(solution)/shard_map/all_to_all | solution.py:541
  20.1 4.8 %copy-start = (s32[1024]{0:T(1024)S(1)}, s32[1024]{0:T(1024)}, u32[]{:S(2)}) copy-start(s32[1024]{0:T(1024)} %param.26) | copy-start | bytes 12292
  20.1 4.8 %copy-start.1 = (s32[1024]{0:T(1024)S(1)}, s32[1024]{0:T(1024)}, u32[]{:S(2)}) copy-start(s32[1024]{0:T(1024)} %param.27) | copy-start | bytes 12292
  20.1 4.8 %copy-start.2 = (s32[256]{0:T(256)S(1)}, s32[256]{0:T(256)}, u32[]{:S(2)}) copy-start(s32[256]{0:T(256)} %param.24) | copy-start | bytes 3076
  20.1 4.8 %copy-start.3 = (s32[256]{0:T(256)S(1)}, s32[256]{0:T(256)}, u32[]{:S(2)}) copy-start(s32[256]{0:T(256)} %param.25) | copy-start | bytes 3076
  20.1 4.8 %copy-start.4 = (s32[1,256]{1,0:T(1,128)S(1)}, s32[1,256]{1,0:T(1,128)}, u32[]{:S(2)}) copy-start(s32[1,256]{1,0:T(1,128)} %bits.1) | copy-start | bytes 3076
  20.1 4.8 %copy-start.5 = (f32[4]{0:T(128)S(1)}, f32[4]{0:T(128)}, u32[]{:S(2)}) copy-start(f32[4]{0:T(128)} %wavelet.1) | copy-start | bytes 52
  20.2 16.3 %collective-permute-start.2 = (f32[632,128]{1,0:T(8,128)S(1)}, f32[632,128]{1,0:T(8,128)S(1)}, u32[]{:S(2)}, u32[]{:S(2)}) collective-permute-start(f32[632,128]{1,0:T(8,128)S(1)} %get-tuple-element.56), channel_id=1, source_target_pairs={{0,16},{16,0},{32,48},{48,32},{64,80},{80,64},{96,112},{112,96},{1... | collective-permute-start | bytes 970760 | tf_op jit(solution)/shard_map/ppermute | solution.py:516
  21.8 14.7 %collective-permute-start.3 = (f32[632,128]{1,0:T(8,128)S(1)}, f32[632,128]{1,0:T(8,128)S(1)}, u32[]{:S(2)}, u32[]{:S(2)}) collective-permute-start(f32[632,128]{1,0:T(8,128)S(1)} %get-tuple-element.57), channel_id=1, source_target_pairs={{16,32},{32,16},{48,64},{64,48},{80,96},{96,80},{17,33},{33,17},{4... | collective-permute-start | bytes 970760 | tf_op jit(solution)/shard_map/ppermute | solution.py:516
  32.9 5.5 %collective-permute-start.4 = (f32[64,128]{1,0:T(8,128)S(1)}, f32[64,128]{1,0:T(8,128)S(1)}, u32[]{:S(2)}, u32[]{:S(2)}) collective-permute-start(f32[64,128]{1,0:T(8,128)S(1)} %get-tuple-element.64), channel_id=1, source_target_pairs={{0,16},{16,0},{32,48},{48,32},{64,80},{80,64},{96,112},{112,96},{1... | collective-permute-start | bytes 98312 | tf_op jit(solution)/shard_map/ppermute | solution.py:516
  40.0 23.6 %all-to-all-start.1 = ((f32[256,2,128]{2,1,0:T(2,128)}), f32[256,2,128]{2,1,0:T(2,128)S(1)}, u32[]{:S(2)}, u32[]{:S(2)}) async-start(f32[256,2,128]{2,1,0:T(2,128)} %bitcast.14), calls=%async_computation.1 | async-start | bytes 524288 | tf_op jit(solution)/shard_map/all_to_all | solution.py:587
  49.3 3.4 %collective-permute-start.5 = (f32[512,128]{1,0:T(8,128)S(1)}, f32[512,128]{1,0:T(8,128)S(1)}, u32[]{:S(2)}, u32[]{:S(2)}) collective-permute-start(f32[512,128]{1,0:T(8,128)S(1)} %get-tuple-element.71), channel_id=1, source_target_pairs={{0,16},{16,0},{32,48},{48,32},{64,80},{80,64},{96,112},{112,96},{1... | collective-permute-start | bytes 786440 | tf_op jit(solution)/shard_map/ppermute | solution.py:516

commit v4 on v3

--- a/solution.py
+++ b/solution.py
@@ -534,7 +534,8 @@
         [HBM] * 8,
         [pltpu.SemaphoreType.DMA((8,))],
     )(*[pltpu.with_memory_space_constraint(a, pltpu.HBM) for a in (*fields, perturbation.reshape(128, 256))])
-    got = (swap(send_e, "ty", 0), swap(send_o, "ty", 1))
+    got_o = swap(send_o, "ty", 1)
+    got = (swap(send_e, "ty", 0), got_o)
     side = pltpu.VMEM((160, NZ), F32)
     blocks = call(pack_windows, shape(704, NZ), [VMEM], [side, side])(plane)
     groups = [[(2 * chip + core) * 16 + ty for chip in range(4) for ty in range(16)] for core in range(2)]
@@ -547,7 +548,8 @@
     )
     strip = shape(*STRIP_X)
     send_e, send_o = call(pack_x, (strip, strip), [VMEM] * 10, cost=BUSY)(*fields, shallow, *got)
-    across = (swap(send_e, "tx", 0), swap(send_o, "tx", 1))
+    across_o = swap(send_o, "tx", 1)
+    across = (swap(send_e, "tx", 0), across_o)
     one = lambda *dims: pltpu.VMEM(dims, F32)
     cells = shape(*tile)
     low = shape(*LOW)

time: 64.9 us -> 64.9 us (level)
  no operation moved by 1% of the time
where the time goes in v4:
time: 64.9 us; the launch traced here: 64.5 us
  starting transfers between devices  34.9 us (54%)
  waiting for transfers between devices  16 us (25%)
  Pallas kernels  12.8 us (20%)
  between operations  0.83 us (1%)
    all_to_all x1, starting transfers between devices, per_device(): lax.all_to_all(blocks.reshape(704, 1, NZ), ('tx', 'ty'), split_axis=0, co...  13.6 us
    ppermute x6, starting transfers between devices, swap(): return lax.ppermute(cells, axis, pairs)  13.4 us
    all_to_all x1, waiting for transfers between devices, per_device(): lax.all_to_all(image.reshape(256, 2, NZ), ('shot', 'tx', 'ty'), split_axi...  8.69 us
    all_to_all x1, starting transfers between devices, per_device(): lax.all_to_all(image.reshape(256, 2, NZ), ('shot', 'tx', 'ty'), split_axi...  7.92 us
    all_to_all x1, waiting for transfers between devices, per_device(): lax.all_to_all(blocks.reshape(704, 1, NZ), ('tx', 'ty'), split_axis=0, co...  6.09 us
    pallas_call x1, Pallas kernels, per_device(): call(born, (cells, cells, cells, cells), [VMEM] * 18, [one(*WIDE)] * 3 +...  2.3 us
    pallas_call x2, Pallas kernels, split(): call(split_windows, (shape(8 * count, NZ),) * 2, [HBM], [one(11 * count +...  2.23 us
    pallas_call x1, Pallas kernels, per_device(): call(free, (shape(STEPS, 3, E, NZ), low, low, low, cells, cells, shape(25...  1.86 us
  transfers between devices with their start and end apart: 8, of which 3 were waited for; matrix products, arithmetic and copies ran while one was open for 0% of the time, Pallas kernels for 14%

profile of v4, /device:TPU:1, one launch (start us, length us, event | category | flops | bytes accessed | tf_op | source)
XLA Modules:
  0.0 64.5 jit_solution(17900208386725930388)
XLA Ops:
  0.6 1.5 %shard_map.173 = (f32[69,8,128]{2,1,0:T(8,128)S(1)}, f32[69,8,128]{2,1,0:T(8,128)S(1)}, f32[80,128]{1,0:T(8,128)S(1)}, f32[16,16,128]{2,1,0:T(8,128)S(1)}, f32[1...) custom-call(f32[16,16,128]{2,1,0:T(8,128)} %bitcast.27, ...), custom_call_target="tpu_custom_call" | custom-call | tf_op jit(solution)/shard_map/pallas_call | solution.py:531
  2.2 2.2 %collective-permute-start = (f32[69,8,128]{2,1,0:T(8,128)S(1)}, f32[69,8,128]{2,1,0:T(8,128)S(1)}, u32[]{:S(2)}, u32[]{:S(2)}) collective-permute-start(f32[69,8,128]{2,1,0:T(8,128)S(1)} %get-tuple-element.54), channel_id=1, source_target_pairs={{0,1},{1,0},{2,3},{3,2},{4,5},{5,4},{6,7},{7,6},{8,9},{9,8},{10,11... | collective-permute-start | bytes 847880 | tf_op jit(solution)/shard_map/ppermute | solution.py:516
  4.4 0.7 %collective-permute-start.1 = (f32[69,8,128]{2,1,0:T(8,128)S(1)}, f32[69,8,128]{2,1,0:T(8,128)S(1)}, u32[]{:S(2)}, u32[]{:S(2)}) collective-permute-start(f32[69,8,128]{2,1,0:T(8,128)S(1)} %get-tuple-element.55), channel_id=1, source_target_pairs={{1,2},{2,1},{3,4},{4,3},{5,6},{6,5},{7,8},{8,7},{9,10},{10,9},{11,... | collective-permute-start | bytes 847880 | tf_op jit(solution)/shard_map/ppermute | solution.py:516
  5.1 1.4 %shard_map.174 = f32[704,128]{1,0:T(8,128)} custom-call(f32[128,256]{1,0:T(8,128)S(1)} %get-tuple-element.42.plane_ref), custom_call_target="tpu_custom_call" | custom-call | tf_op jit(solution)/shard_map/pallas_call | solution.py:540
  6.5 13.6 %all-to-all-start = ((f32[704,1,128]{2,1,0:T(1,128)}), f32[704,1,128]{2,1,0:T(1,128)}, u32[]{:S(2)}, u32[]{:S(2)}) async-start(f32[704,1,128]{2,1,0:T(1,128)} %bitcast.8), calls=%async_computation | async-start | bytes 720896 | tf_op jit(solution)/shard_map/all_to_all | solution.py:542
  20.1 0.0 collective-permute-done.refs_8_.refs_7_
  20.1 0.0 collective-permute-done.1.refs_9_.refs_8_
  20.1 0.0 copy-start
  20.1 0.0 copy-start.1
  20.1 0.0 copy-start.2
  20.1 0.0 copy-start.3
  20.1 0.0 copy-start.4
  20.1 0.0 copy-start.5
  20.1 0.1 shard_map.176
  20.2 1.6 %collective-permute-start.2 = (f32[632,128]{1,0:T(8,128)S(1)}, f32[632,128]{1,0:T(8,128)S(1)}, u32[]{:S(2)}, u32[]{:S(2)}) collective-permute-start(f32[632,128]{1,0:T(8,128)S(1)} %get-tuple-element.56), channel_id=1, source_target_pairs={{0,16},{16,0},{32,48},{48,32},{64,80},{80,64},{96,112},{112,96},{1... | collective-permute-start | bytes 970760 | tf_op jit(solution)/shard_map/ppermute | solution.py:516
  21.8 3.0 %collective-permute-start.3 = (f32[632,128]{1,0:T(8,128)S(1)}, f32[632,128]{1,0:T(8,128)S(1)}, u32[]{:S(2)}, u32[]{:S(2)}) collective-permute-start(f32[632,128]{1,0:T(8,128)S(1)} %get-tuple-element.57), channel_id=1, source_target_pairs={{16,32},{32,16},{48,64},{64,48},{80,96},{96,80},{17,33},{33,17},{4... | collective-permute-start | bytes 970760 | tf_op jit(solution)/shard_map/ppermute | solution.py:516
  24.9 1.0 %shard_map.175 = (f32[3,32,128]{2,1,0:T(8,128)S(1)}, f32[3,32,128]{2,1,0:T(8,128)S(1)}, f32[8,128]{1,0:T(8,128)S(1)}) custom-call(f32[4]{0:T(128)S(1)} %copy-done.5, s32[1,256]{1,0:T(1,128)S(1)} %bitcast.25, s32[1,256]{1,0:T(1,128)S(1)} %bitcast.26, s32[1,256]{1,0:T(1,128)S(1)} %copy-done.4, s32[1,1024]{1,0:T(1,128)S(1)} %bitcast.23, s32[1,1024]{1,0:T(1,128)S(1)} %bitcast.24), custom_call_target="tpu_custom_call" | custom-call | tf_op jit(solution)/shard_map/pallas_call | solution.py:546
  25.9 6.1 %all-to-all-done = f32[704,1,128]{2,1,0:T(1,128)} async-done(((f32[704,1,128]{2,1,0:T(1,128)}), f32[704,1,128]{2,1,0:T(1,128)}, u32[]{:S(2)}, u32[]{:S(2)}) %all-to-all-start) | async-done | bytes 360480 | tf_op jit(solution)/shard_map/all_to_all | solution.py:542
  32.0 0.9 %shard_map.178 = (f32[64,128]{1,0:T(8,128)S(1)}, f32[64,128]{1,0:T(8,128)S(1)}) custom-call(f32[704,128]{1,0:T(8,128)} %bitcast.9.source), custom_call_target="tpu_custom_call" | custom-call | tf_op jit(solution)/shard_map/pallas_call | solution.py:565
  32.9 3.6 %collective-permute-start.4 = (f32[64,128]{1,0:T(8,128)S(1)}, f32[64,128]{1,0:T(8,128)S(1)}, u32[]{:S(2)}, u32[]{:S(2)}) collective-permute-start(f32[64,128]{1,0:T(8,128)S(1)} %get-tuple-element.64), channel_id=1, source_target_pairs={{0,16},{16,0},{32,48},{48,32},{64,80},{80,64},{96,112},{112,96},{1... | collective-permute-start | bytes 98312 | tf_op jit(solution)/shard_map/ppermute | solution.py:516
  36.5 0.0 collective-permute-done.2.refs_10_.refs_9_
  36.5 0.0 collective-permute-done.3.refs_11_.refs_10_
  36.5 1.9 %shard_map.177 = (f32[4,3,32,128]{3,2,1,0:T(8,128)S(1)}, f32[3,48,128]{2,1,0:T(8,128)S(1)}, f32[3,48,128]{2,1,0:T(8,128)S(1)}, f32[3,48,128]{2,1,0:T(8,128)S(1)}...) custom-call(f32[8,128]{1,0:T(8,128)S(1)} %get-tuple-element.45.scales, ...), custom_call_target="tpu_custom_call" | custom-call | tf_op jit(solution)/shard_map/pallas_call | solution.py:556
  38.4 0.0 collective-permute-done.4.got
  38.4 1.6 %shard_map.179 = (f32[512,128]{1,0:T(8,128)}, f32[2,16,128]{2,1,0:T(8,128)S(1)}) custom-call(f32[4,3,32,128]{3,2,1,0:T(8,128)S(1)} %get-tuple-element.58.SA, f32[3,48,128]{2,1,0:T(8,128)S(1)} %get-tuple-element.59.CS, f32[3,48,128]{2,1,0:T(8,128)S(1)} %get-tuple-element.60.BS0, f32[3,48,128]{2,1,0:T(8,128)S(1)} %get-tuple-element.61.BS1, ...), custom_call_target="tpu_custom_call" | custom-call | tf_op jit(solution)/shard_map/pallas_call | solution.py:572
  40.0 7.9 %all-to-all-start.1 = ((f32[256,2,128]{2,1,0:T(2,128)}), f32[256,2,128]{2,1,0:T(2,128)S(1)}, u32[]{:S(2)}, u32[]{:S(2)}) async-start(f32[256,2,128]{2,1,0:T(2,128)} %bitcast.14), calls=%async_computation.1 | async-start | bytes 524288 | tf_op jit(solution)/shard_map/all_to_all | solution.py:589
  47.9 1.3 %shard_map.181 = (f32[512,128]{1,0:T(8,128)S(1)}, f32[512,128]{1,0:T(8,128)S(1)}) custom-call(f32[704,128]{1,0:T(8,128)} %bitcast.9.source), custom_call_target="tpu_custom_call" | custom-call | tf_op jit(solution)/shard_map/pallas_call | solution.py:565
  49.3 2.2 %collective-permute-start.5 = (f32[512,128]{1,0:T(8,128)S(1)}, f32[512,128]{1,0:T(8,128)S(1)}, u32[]{:S(2)}, u32[]{:S(2)}) collective-permute-start(f32[512,128]{1,0:T(8,128)S(1)} %get-tuple-element.71), channel_id=1, source_target_pairs={{0,16},{16,0},{32,48},{48,32},{64,80},{80,64},{96,112},{112,96},{1... | collective-permute-start | bytes 786440 | tf_op jit(solution)/shard_map/ppermute | solution.py:516
  51.5 1.2 %collective-permute-done.5.refs_13_ = f32[512,128]{1,0:T(8,128)S(1)} collective-permute-done((f32[512,128]{1,0:T(8,128)S(1)}, f32[512,128]{1,0:T(8,128)S(1)}, u32[]{:S(2)}, u32[]{:S(2)}) %collective-permute-start.5) | collective-permute-done | bytes 262176 | tf_op jit(solution)/shard_map/ppermute | solution.py:516
  52.7 2.3 %shard_map.182 = (f32[16,16,128]{2,1,0:T(8,128)}, f32[16,16,128]{2,1,0:T(8,128)}, f32[16,16,128]{2,1,0:T(8,128)}, f32[16,16,128]{2,1,0:T(8,128)}) custom-call(f32[8,128]{1,0:T(8,128)S(1)} %get-tuple-element.45.scales, f32[16,16,128]{2,1,0:T(8,128)S(1)} %get-tuple-element.46.refs_0_, f32[16,16,128]{2,1,0:T(8,128)S(1)} %get-tuple-element.47.refs_1_, ...), custom_call_target="tpu_custom_call" | custom-call | tf_op jit(solution)/shard_map/pallas_call | solution.py:582
  55.0 8.7 %all-to-all-done.1 = f32[256,2,128]{2,1,0:T(2,128)S(1)} async-done(((f32[256,2,128]{2,1,0:T(2,128)}), f32[256,2,128]{2,1,0:T(2,128)S(1)}, u32[]{:S(2)}, u32[]{:S(2)}) %all-to-all-start.1) | async-done | bytes 262176 | tf_op jit(solution)/shard_map/all_to_all | solution.py:589
  63.7 0.8 %shard_map.180 = f32[128,128]{1,0:T(8,128)} custom-call(f32[512,128]{1,0:T(8,128)S(1)} %bitcast.22), custom_call_target="tpu_custom_call" | custom-call | tf_op jit(solution)/shard_map/pallas_call | solution.py:592
  (6 shorter events, 0.0 us)
Async XLA Ops:
  2.2 17.9 %collective-permute-start = (f32[69,8,128]{2,1,0:T(8,128)S(1)}, f32[69,8,128]{2,1,0:T(8,128)S(1)}, u32[]{:S(2)}, u32[]{:S(2)}) collective-permute-start(f32[69,8,128]{2,1,0:T(8,128)S(1)} %get-tuple-element.54), channel_id=1, source_target_pairs={{0,1},{1,0},{2,3},{3,2},{4,5},{5,4},{6,7},{7,6},{8,9},{9,8},{10,11... | collective-permute-start | bytes 847880 | tf_op jit(solution)/shard_map/ppermute | solution.py:516
  4.4 15.7 %collective-permute-start.1 = (f32[69,8,128]{2,1,0:T(8,128)S(1)}, f32[69,8,128]{2,1,0:T(8,128)S(1)}, u32[]{:S(2)}, u32[]{:S(2)}) collective-permute-start(f32[69,8,128]{2,1,0:T(8,128)S(1)} %get-tuple-element.55), channel_id=1, source_target_pairs={{1,2},{2,1},{3,4},{4,3},{5,6},{6,5},{7,8},{8,7},{9,10},{10,9},{11,... | collective-permute-start | bytes 847880 | tf_op jit(solution)/shard_map/ppermute | solution.py:516
  6.5 25.5 %all-to-all-start = ((f32[704,1,128]{2,1,0:T(1,128)}), f32[704,1,128]{2,1,0:T(1,128)}, u32[]{:S(2)}, u32[]{:S(2)}) async-start(f32[704,1,128]{2,1,0:T(1,128)} %bitcast.8), calls=%async_computation | async-start | bytes 720896 | tf_op jit(solution)/shard_map/all_to_all | solution.py:542
  20.1 4.8 %copy-start = (s32[1024]{0:T(1024)S(1)}, s32[1024]{0:T(1024)}, u32[]{:S(2)}) copy-start(s32[1024]{0:T(1024)} %param.26) | copy-start | bytes 12292
  20.1 4.8 %copy-start.1 = (s32[1024]{0:T(1024)S(1)}, s32[1024]{0:T(1024)}, u32[]{:S(2)}) copy-start(s32[1024]{0:T(1024)} %param.27) | copy-start | bytes 12292
  20.1 4.8 %copy-start.2 = (s32[256]{0:T(256)S(1)}, s32[256]{0:T(256)}, u32[]{:S(2)}) copy-start(s32[256]{0:T(256)} %param.24) | copy-start | bytes 3076
  20.1 4.8 %copy-start.3 = (s32[256]{0:T(256)S(1)}, s32[256]{0:T(256)}, u32[]{:S(2)}) copy-start(s32[256]{0:T(256)} %param.25) | copy-start | bytes 3076
  20.1 4.8 %copy-start.4 = (s32[1,256]{1,0:T(1,128)S(1)}, s32[1,256]{1,0:T(1,128)}, u32[]{:S(2)}) copy-start(s32[1,256]{1,0:T(1,128)} %bits.1) | copy-start | bytes 3076
  20.1 4.8 %copy-start.5 = (f32[4]{0:T(128)S(1)}, f32[4]{0:T(128)}, u32[]{:S(2)}) copy-start(f32[4]{0:T(128)} %wavelet.1) | copy-start | bytes 52
  20.2 16.3 %collective-permute-start.2 = (f32[632,128]{1,0:T(8,128)S(1)}, f32[632,128]{1,0:T(8,128)S(1)}, u32[]{:S(2)}, u32[]{:S(2)}) collective-permute-start(f32[632,128]{1,0:T(8,128)S(1)} %get-tuple-element.56), channel_id=1, source_target_pairs={{0,16},{16,0},{32,48},{48,32},{64,80},{80,64},{96,112},{112,96},{1... | collective-permute-start | bytes 970760 | tf_op jit(solution)/shard_map/ppermute | solution.py:516
  21.8 14.7 %collective-permute-start.3 = (f32[632,128]{1,0:T(8,128)S(1)}, f32[632,128]{1,0:T(8,128)S(1)}, u32[]{:S(2)}, u32[]{:S(2)}) collective-permute-start(f32[632,128]{1,0:T(8,128)S(1)} %get-tuple-element.57), channel_id=1, source_target_pairs={{16,32},{32,16},{48,64},{64,48},{80,96},{96,80},{17,33},{33,17},{4... | collective-permute-start | bytes 970760 | tf_op jit(solution)/shard_map/ppermute | solution.py:516
  32.9 5.5 %collective-permute-start.4 = (f32[64,128]{1,0:T(8,128)S(1)}, f32[64,128]{1,0:T(8,128)S(1)}, u32[]{:S(2)}, u32[]{:S(2)}) collective-permute-start(f32[64,128]{1,0:T(8,128)S(1)} %get-tuple-element.64), channel_id=1, source_target_pairs={{0,16},{16,0},{32,48},{48,32},{64,80},{80,64},{96,112},{112,96},{1... | collective-permute-start | bytes 98312 | tf_op jit(solution)/shard_map/ppermute | solution.py:516
  40.0 23.6 %all-to-all-start.1 = ((f32[256,2,128]{2,1,0:T(2,128)}), f32[256,2,128]{2,1,0:T(2,128)S(1)}, u32[]{:S(2)}, u32[]{:S(2)}) async-start(f32[256,2,128]{2,1,0:T(2,128)} %bitcast.14), calls=%async_computation.1 | async-start | bytes 524288 | tf_op jit(solution)/shard_map/all_to_all | solution.py:589
  49.3 3.4 %collective-permute-start.5 = (f32[512,128]{1,0:T(8,128)S(1)}, f32[512,128]{1,0:T(8,128)S(1)}, u32[]{:S(2)}, u32[]{:S(2)}) collective-permute-start(f32[512,128]{1,0:T(8,128)S(1)} %get-tuple-element.71), channel_id=1, source_target_pairs={{0,16},{16,0},{32,48},{48,32},{64,80},{80,64},{96,112},{112,96},{1... | collective-permute-start | bytes 786440 | tf_op jit(solution)/shard_map/ppermute | solution.py:516
